TPU v7x, 128 devices: a whole 4x4x4 slice. The times are simulated.
128 devices in a mesh: dp: 8 (over z, core), seq: 4 (over y), head: 4 (over x).
Axes of the slice: x: 4, y: 4, z: 4, core: 2. Of those that a mesh axis runs over, the one named last changes fastest.
Arguments:
- tokens: bfloat16 [16, 1024, 2048], P('dp', ('seq', 'head')), may hold values from -6 to 6
- w_qkv: bfloat16 [2048, 2688], replicated, may hold values from -0.125 to 0.125
- w_out: bfloat16 [1792, 2048], replicated, may hold values from -1 to 1
- w_ffn_in: bfloat16 [7168, 2, 2048], P(('seq', 'head')), may hold values from -0.125 to 0.125
- w_ffn_out: bfloat16 [7168, 2048], P(('seq', 'head')), may hold values from -0.0625 to 0.0625
- g_attn: float32 [2048], replicated, may hold values from 0.5 to 1.5
- g_ffn: float32 [2048], replicated, may hold values from 0.5 to 1.5
- q_gain: float32 [64], replicated, may hold values from 0.1 to 1.9
- k_gain: float32 [64], replicated, may hold values from 0.1 to 1.9
- doc_starts: int32 [16, 4], P('dp'), may hold values from 0 to 1023, as said below
- d_out: bfloat16 [16, 1024, 2048], P('dp', ('seq', 'head')), may hold values from -6 to 6
Outputs:
- output: bfloat16 [16, 1024, 2048], P('dp', ('seq', 'head'))
- grad_tokens: bfloat16 [16, 1024, 2048], P('dp', ('seq', 'head'))
- grad_w_qkv: float32 [2048, 2688], P(('dp', 'seq', 'head'))
- grad_w_out: float32 [1792, 2048], P(None, ('dp', 'seq', 'head'))
- grad_w_ffn_in: float32 [7168, 2, 2048], P(('seq', 'head'))
- grad_w_ffn_out: float32 [7168, 2048], P(('seq', 'head'))
- grad_g_attn: float32 [2048], replicated
- grad_g_ffn: float32 [2048], replicated
- grad_q_gain: float32 [64], replicated
- grad_k_gain: float32 [64], replicated
Inputs may be any that keep to these rules, and one draw needn't show every extreme that they name: `doc_starts`: each row holds 4 documents; its offsets rise and the first is 0. In every row one document begins within the first 256 positions and ends within the last 256.
All inputs are finite; a program needn't handle non-finite values.
Results may differ from a plain program's by a relative error of at most 0.02.
Values may be sent and summed in bfloat16 or wider, within the bound.
A program may use at most 256 MiB of HBM per device.

v0:
```python
import math

import jax
import jax.numpy as jnp
from jax import lax
from jax.sharding import Mesh
from jax.sharding import PartitionSpec as P

HEADS = 28
KV = 7
HD = 64
DP_SEQ_HEAD = ("dp_0", "dp_1", "seq", "head")
DP = ("dp_0", "dp_1")


EPS = 1e-06
SCALE = 0.125
NEGATIVE = -1e30


def joined_along(pieces, dim):
    lengths = list(pieces.shape[1:])
    lengths[dim] *= pieces.shape[0]
    return jnp.moveaxis(pieces, 0, dim).reshape(lengths)


def copy_for_each(array, axis):
    copies = jnp.broadcast_to(array, (lax.axis_size(axis), *array.shape))
    return lax.all_to_all(copies, axis, split_axis=0, concat_axis=0, tiled=True)


def collect(array, axis, dim):
    return joined_along(copy_for_each(array, axis), dim)


def in_blocks(array, dim, peers):
    lengths = array.shape
    pieces = array.reshape(*lengths[:dim], peers, lengths[dim] // peers, *lengths[dim + 1 :])
    return jnp.moveaxis(pieces, dim, 0)


def sum_at_owner(array, axis, dim):
    peers = lax.axis_size(axis)
    pieces = lax.all_to_all(in_blocks(array, dim, peers), axis, 0, 0, tiled=True)
    return jnp.sum(pieces.astype(jnp.float32), axis=0)


def one_axis_at_a_time(array, axes):
    for axis in axes:
        array = lax.psum(array, axis)
    return array


def rms_parts(v):
    inverse = lax.rsqrt(jnp.mean(v * v, axis=-1, keepdims=True) + EPS)
    return (v * inverse, inverse)


def rms_back(grad, normed, inverse):
    return inverse * (grad - normed * jnp.mean(grad * normed, axis=-1, keepdims=True))


def rotate(v, cosine, sine):
    half = v.shape[-1] // 2
    first = v[..., :half]
    second = v[..., half:]
    return jnp.concatenate([first * cosine - second * sine, second * cosine + first * sine], -1)


def angle_tables(positions, width):
    half = width // 2
    freq = jnp.exp(jnp.arange(half, dtype=jnp.float32) * (-2.0 * math.log(10000.0) / width))
    angle = positions.astype(jnp.float32)[:, None] * freq[None, :]
    return (jnp.cos(angle), jnp.sin(angle))


def slot_table(groups, slots, devices):
    index = jnp.arange(groups)
    owner = index % devices
    rank = index // devices
    place = owner * slots + rank
    return (place[None, :] == jnp.arange(devices * slots)[:, None]).astype(jnp.bfloat16)


def body(
    tokens, w_qkv, w_out, w_ffn_in, w_ffn_out, g_attn, g_ffn, q_gain, k_gain, doc_starts, d_out
):
    f32 = jnp.float32
    bf16 = jnp.bfloat16
    rows, tok, width = tokens.shape
    n_seq = lax.axis_size("seq")
    n_head = lax.axis_size("head")
    span = tok * n_head
    length = span * n_seq
    per_group = HEADS // KV
    slots = (KV + n_head - 1) // n_head
    q_cols = per_group * HD
    table = slot_table(KV, slots, n_head)
    seq_index = lax.axis_index("seq")
    head_index = lax.axis_index("head")
    tok_pos = seq_index * span + head_index * tok + jnp.arange(tok)
    cosine, sine = angle_tables(tok_pos, HD)
    cosine = cosine[None, :, None, :]
    sine = sine[None, :, None, :]
    xf = tokens.astype(f32)
    n1, inv1 = rms_parts(xf)
    h1 = (n1 * g_attn).astype(bf16)
    qkv = jnp.einsum("rtd,dk->rtk", h1, w_qkv, preferred_element_type=f32)
    q_raw = qkv[..., : HEADS * HD].reshape(rows, tok, HEADS, HD)
    k_raw = qkv[..., HEADS * HD : (HEADS + KV) * HD].reshape(rows, tok, KV, HD)
    v_raw = qkv[..., (HEADS + KV) * HD :].reshape(rows, tok, KV, HD)
    q_normed, inv_q = rms_parts(q_raw)
    k_normed, inv_k = rms_parts(k_raw)
    q_rot = rotate(q_normed * q_gain, cosine, sine)
    k_rot = rotate(k_normed * k_gain, cosine, sine)
    packed = jnp.concatenate([q_rot.reshape(rows, tok, KV, q_cols), k_rot, v_raw], -1).astype(bf16)
    by_slot = jnp.einsum("rtgc,sg->rtsc", packed, table, preferred_element_type=f32).astype(bf16)
    local = lax.all_to_all(by_slot, "head", split_axis=2, concat_axis=1, tiled=True)
    queries = local[..., :q_cols].reshape(rows, span, slots, per_group, HD)
    key_value = collect(local[..., q_cols:], "seq", 1)
    q_pos = seq_index * span + jnp.arange(span)
    all_pos = jnp.arange(length)
    ids_all = jnp.sum((doc_starts[:, None, :] <= all_pos[None, :, None]).astype(jnp.int32), axis=2)
    ids_q = lax.dynamic_slice_in_dim(ids_all, seq_index * span, span, 1)

    def block_mask(block):
        k_pos = block * span + jnp.arange(span)
        ids_k = ids_all[:, block * span : (block + 1) * span]
        causal = k_pos[None, :] <= q_pos[:, None]
        same = ids_q[:, :, None] == ids_k[:, None, :]
        return (causal[None] & same)[:, None, None]

    best = jnp.full((rows, slots, per_group, span), NEGATIVE, f32)
    total = jnp.zeros((rows, slots, per_group, span), f32)
    accum = jnp.zeros((rows, slots, per_group, span, HD), f32)
    state = (best, total, accum)
    for block in range(n_seq):
        keys_b = key_value[:, block * span : (block + 1) * span, :, :HD]
        vals_b = key_value[:, block * span : (block + 1) * span, :, HD:]
        mask = block_mask(block)

        def attend(carried, keys_b=keys_b, vals_b=vals_b, mask=mask):
            old_best, old_total, old_accum = carried
            scores = (
                jnp.einsum("rqsha,rksa->rshqk", queries, keys_b, preferred_element_type=f32) * SCALE
            )
            scores = jnp.where(mask, scores, NEGATIVE)
            new_best = jnp.maximum(old_best, jnp.max(scores, -1))
            factor = jnp.exp(old_best - new_best)
            probs = jnp.where(mask, jnp.exp(scores - new_best[..., None]), 0.0)
            new_total = old_total * factor + jnp.sum(probs, -1)
            new_accum = old_accum * factor[..., None] + jnp.einsum(
                "rshqk,rksa->rshqa", probs.astype(bf16), vals_b, preferred_element_type=f32
            )
            return (new_best, new_total, new_accum)

        state = attend(state)
    best, total, accum = state
    attn_o = accum / total[..., None]
    log_total = best + jnp.log(total)
    o_send = attn_o.astype(bf16).transpose(0, 3, 1, 2, 4).reshape(rows, span, slots, q_cols)
    o_back = lax.all_to_all(o_send, "head", split_axis=1, concat_axis=2, tiled=True)
    o_tok = jnp.einsum("rtsc,sg->rtgc", o_back, table, preferred_element_type=f32).astype(bf16)
    o_tok = o_tok.reshape(rows, tok, HEADS * HD)
    attn = jnp.einsum("rtk,kd->rtd", o_tok, w_out, preferred_element_type=f32)
    r1 = xf + attn
    n2, inv2 = rms_parts(r1)
    h2 = (n2 * g_ffn).astype(bf16)
    h2_all = lax.all_gather(
        h2.reshape(1, rows * tok, width), ("seq", "head"), axis=0, tiled=True
    ).reshape(-1, width)
    both = jnp.einsum("fcd,td->fct", w_ffn_in, h2_all, preferred_element_type=f32)
    gate = both[:, 0]
    up = both[:, 1]
    sig = jax.nn.sigmoid(gate)
    act = gate * sig
    hidden = (act * up).astype(bf16)
    part = hidden
    ffn = (
        lax.psum_scatter(
            jnp.einsum("ft,fd->td", part, w_ffn_out, preferred_element_type=f32).astype(
                jnp.bfloat16
            ),
            ("seq", "head"),
            scatter_dimension=0,
            tiled=True,
        )
        .astype(jnp.float32)
        .reshape(rows, tok, width)
    )
    output = (r1 + ffn).astype(bf16)
    dy_all = lax.all_gather(
        d_out.reshape(1, rows * tok, width), ("seq", "head"), axis=0, tiled=True
    ).reshape(-1, width)
    d_hidden = jnp.einsum("fd,td->ft", w_ffn_out, dy_all, preferred_element_type=f32)
    grad_down = jnp.einsum("ft,td->fd", hidden, dy_all, preferred_element_type=f32)
    d_gate = d_hidden * up * (sig * (1.0 + gate * (1.0 - sig)))
    d_up = d_hidden * act
    d_both = jnp.stack([d_gate, d_up], 1).astype(bf16)
    grad_in = jnp.einsum("fct,td->fcd", d_both, h2_all, preferred_element_type=f32)
    part = d_both
    d_h2 = (
        lax.psum_scatter(
            jnp.einsum("fct,fcd->td", part, w_ffn_in, preferred_element_type=f32).astype(
                jnp.bfloat16
            ),
            ("seq", "head"),
            scatter_dimension=0,
            tiled=True,
        )
        .astype(jnp.float32)
        .reshape(rows, tok, width)
    )
    grad_gffn = jnp.sum(d_h2 * n2, axis=(0, 1))
    d_r1 = d_out.astype(f32) + rms_back(d_h2 * g_ffn, n2, inv2)
    d_attn = d_r1.astype(bf16)
    d_o = jnp.einsum("rtd,kd->rtk", d_attn, w_out, preferred_element_type=f32).astype(bf16)
    d_o_slots = jnp.einsum(
        "rtgc,sg->rtsc", d_o.reshape(rows, tok, KV, q_cols), table, preferred_element_type=f32
    ).astype(bf16)
    d_local = lax.all_to_all(d_o_slots, "head", split_axis=2, concat_axis=1, tiled=True)
    d_o_heads = d_local.reshape(rows, span, slots, per_group, HD).transpose(0, 2, 3, 1, 4)
    delta = jnp.sum(d_o_heads.astype(f32) * attn_o, -1)
    d_query = jnp.zeros((rows, slots, per_group, span, HD), f32)
    key_grads = []
    for block in range(n_seq):
        keys_b = key_value[:, block * span : (block + 1) * span, :, :HD]
        vals_b = key_value[:, block * span : (block + 1) * span, :, HD:]
        mask = block_mask(block)

        def backward(carried, keys_b=keys_b, vals_b=vals_b, mask=mask):
            scores = (
                jnp.einsum("rqsha,rksa->rshqk", queries, keys_b, preferred_element_type=f32) * SCALE
            )
            probs = jnp.where(mask, jnp.exp(scores - log_total[..., None]), 0.0)
            d_probs = jnp.einsum("rshqa,rksa->rshqk", d_o_heads, vals_b, preferred_element_type=f32)
            d_vals = jnp.einsum(
                "rshqk,rshqa->rksa", probs.astype(bf16), d_o_heads, preferred_element_type=f32
            )
            d_scores = (probs * (d_probs - delta[..., None])).astype(bf16)
            new_query = (
                carried
                + jnp.einsum("rshqk,rksa->rshqa", d_scores, keys_b, preferred_element_type=f32)
                * SCALE
            )
            d_keys = (
                jnp.einsum("rshqk,rqsha->rksa", d_scores, queries, preferred_element_type=f32)
                * SCALE
            )
            return (new_query, jnp.concatenate([d_keys, d_vals], -1))

        d_query, block_grad = backward(d_query)
        key_grads.append(block_grad)
    kv_terms = jnp.concatenate(key_grads, 1)
    d_kv = sum_at_owner(kv_terms.astype(jnp.bfloat16), "seq", 1).astype(bf16)
    d_q = d_query.astype(bf16).transpose(0, 3, 1, 2, 4).reshape(rows, span, slots, q_cols)
    d_send = jnp.concatenate([d_q, d_kv], -1)
    d_back = lax.all_to_all(d_send, "head", split_axis=1, concat_axis=2, tiled=True)
    d_packed = jnp.einsum("rtsc,sg->rtgc", d_back, table, preferred_element_type=f32)
    d_qrot = d_packed[..., :q_cols].reshape(rows, tok, HEADS, HD)
    d_krot = d_packed[..., q_cols : q_cols + HD]
    d_vraw = d_packed[..., q_cols + HD :]
    d_qs = rotate(d_qrot, cosine, -sine)
    d_ks = rotate(d_krot, cosine, -sine)
    grad_qgain = jnp.sum(d_qs * q_normed, axis=(0, 1, 2))
    grad_kgain = jnp.sum(d_ks * k_normed, axis=(0, 1, 2))
    d_qraw = rms_back(d_qs * q_gain, q_normed, inv_q)
    d_kraw = rms_back(d_ks * k_gain, k_normed, inv_k)
    d_qkv = jnp.concatenate(
        [
            d_qraw.reshape(rows, tok, HEADS * HD),
            d_kraw.reshape(rows, tok, KV * HD),
            d_vraw.reshape(rows, tok, KV * HD),
        ],
        -1,
    ).astype(bf16)
    d_h1 = jnp.einsum("rtk,dk->rtd", d_qkv, w_qkv, preferred_element_type=f32)
    grad_gattn = jnp.sum(d_h1 * n1, axis=(0, 1))
    grad_x = (d_r1 + rms_back(d_h1 * g_attn, n1, inv1)).astype(bf16)
    left = jnp.einsum("rtd,rtk->dk", h1, d_qkv, preferred_element_type=f32)
    right = jnp.einsum("rtd,rtk->dk", d_attn, o_tok, preferred_element_type=f32)
    weight_part = lax.psum_scatter(
        jnp.concatenate([left, right], 1), DP_SEQ_HEAD, scatter_dimension=0, tiled=True
    )
    qkv_width = w_qkv.shape[1]
    grad_qkv = weight_part[:, :qkv_width]
    grad_out = weight_part[:, qkv_width:].T
    grad_in_sum, grad_down_sum = (
        lax.psum(grad_in.astype(jnp.bfloat16), DP).astype(jnp.float32),
        lax.psum(grad_down.astype(jnp.bfloat16), DP).astype(jnp.float32),
    )
    gain_attn, gain_ffn, gain_q, gain_k = (
        one_axis_at_a_time(grad_gattn, DP_SEQ_HEAD),
        one_axis_at_a_time(grad_gffn, DP_SEQ_HEAD),
        one_axis_at_a_time(grad_qgain, DP_SEQ_HEAD),
        one_axis_at_a_time(grad_kgain, DP_SEQ_HEAD),
    )
    return (
        output,
        grad_x,
        grad_qkv,
        grad_out,
        grad_in_sum,
        grad_down_sum,
        gain_attn,
        gain_ffn,
        gain_q,
        gain_k,
    )


def solution(mesh):
    split = Mesh(
        mesh.devices.reshape(4, 2, mesh.shape["seq"], mesh.shape["head"]),
        ("dp_0", "dp_1", "seq", "head"),
    )
    return jax.shard_map(
        body,
        mesh=split,
        in_specs=(
            P(DP, ("seq", "head"), None),
            P(),
            P(),
            P(("seq", "head"), None, None),
            P(("seq", "head"), None),
            P(),
            P(),
            P(),
            P(),
            P(DP, None),
            P(DP, ("seq", "head"), None),
        ),
        out_specs=(
            P(DP, ("seq", "head"), None),
            P(DP, ("seq", "head"), None),
            P(DP_SEQ_HEAD, None),
            P(None, DP_SEQ_HEAD),
            P(("seq", "head"), None, None),
            P(("seq", "head"), None),
            P(),
            P(),
            P(),
            P(),
        ),
        check_vma=False,
    )
```

profile of v0, /device:TPU:0, one launch (start us, length us, event | category | flops | bytes accessed | tf_op | source)
XLA Modules:
  0.0 1340.5 jit_solution(15453813465843525050)
XLA Ops:
  8.6 6.0 fusion.2
  29.9 4.4 all-to-all-start
  34.4 12.2 all-to-all-done
  48.8 4.5 all-to-all-start.1
  58.1 9.1 all-to-all-done.1
  84.0 10.5 all_to_all.79
  99.9 4.5 multiply_reduce_fusion.3
  107.2 68.5 %all-gather.3.cloned.1.call-done = bf16[16,128,2048]{2,1,0:T(8,128)(2,1)} async-done(((bf16[1,128,2048]{2,1,0:T(8,128)(2,1)}), bf16[16,128,2048]{2,1,0:T(8,128)(2,1)}) %all-gather.3.cloned.1.call-update) | async-done | bytes 8388624 | tf_op jit(solution)/shard_map/all_gather | solution.py:169
  175.7 14.2 %convolution_bitcast_fusion.2 = f32[448,2,2048]{2,0,1:T(8,128)} fusion(bf16[2048,2048,1]{1,0,2:T(8,128)(2,1)} %bitcast.577, bf16[448,2,2048]{2,1,0:T(2,128)(2,1)} %param.14), kind=kOutput, calls=%fused_computation.37 | convolution fusion | flops 7516192768 | bytes 19398656 | tf_op jit(solution)/shard_map/fcd,td->fct/dot_general | solution.py:172
  189.9 58.3 %all-gather.5.cloned.1.call-done = bf16[16,128,2048]{2,1,0:T(8,128)(2,1)} async-done(((bf16[1,128,2048]{2,1,0:T(8,128)(2,1)}), bf16[16,128,2048]{2,1,0:T(8,128)(2,1)}) %all-gather.5.cloned.1.call-update) | async-done | bytes 8388624 | tf_op jit(solution)/shard_map/all_gather | solution.py:192
  248.2 10.9 fusion.75
  260.9 11.7 bitcast_convert_fusion
  272.7 10.3 convolution_convert_fusion
  291.6 65.9 %reduce-scatter.6.cloned.1.call-done = bf16[128,2048]{1,0:T(8,128)(2,1)} async-done(((bf16[2048,2048]{1,0:T(8,128)(2,1)}), bf16[128,2048]{1,0:T(8,128)(2,1)}) %reduce-scatter.6.cloned.1.call-update) | async-done | bytes 524304 | tf_op jit(solution)/shard_map/reduce_scatter | solution.py:203
  359.8 85.5 %reduce-scatter.4.cloned.1.call-done = bf16[128,2048]{1,0:T(8,128)(2,1)} async-done(((bf16[2048,2048]{1,0:T(8,128)(2,1)}), bf16[128,2048]{1,0:T(8,128)(2,1)}) %reduce-scatter.4.cloned.1.call-update) | async-done | bytes 524304 | tf_op jit(solution)/shard_map/reduce_scatter | solution.py:180
  447.7 5.6 fusion.45
  455.2 3.9 all-to-all-start.3
  459.1 13.1 convolution_convert_fusion.1
  494.2 4.7 all-to-all-start.4
  505.2 7.5 all-to-all-done.4
  516.0 4.5 all-to-all-start.5
  520.5 10.8 convolution_convert_fusion.2
  532.3 7.4 convolution_bitcast_fusion.1
  571.1 9.2 convolution_bitcast_fusion
  580.3 25.9 %pad_maximum_fusion = f32[2048,4480]{1,0:T(8,128)} fusion(f32[2048,1792]{1,0:T(8,128)} %convolution_bitcast_fusion.1, f32[2048,2688]{1,0:T(8,128)} %convolution_bitcast_fusion), kind=kLoop, calls=%fused_computation | loop fusion | flops 9175040 | bytes 73400320 | tf_op jit(solution)/shard_map/concatenate | solution.py:283
  606.2 4.1 all-reduce.7.cloned.1.call-done
  610.3 9.1 copy.214
  621.9 9.1 fusion.145
  631.0 15.2 %all-reduce.2 = (f32[2048]{0:T(1024)S(1)}, f32[2048]{0:T(1024)S(1)}, f32[64]{0:T(128)S(1)}, f32[64]{0:T(128)S(1)}) all-reduce(f32[2048]{0:T(1024)S(1)} %get-tuple-element.60, f32[2048]{0:T(1024)S(1)} %copy-done.80, f32[64]{0:T(128)S(1)} %reduce_sum.219, ...), channel_id=1, replica_groups=mesh['dp_0'=4,'dp_1'=2,'seq'=4,'head'=4] {'dp_0'}, use_global_device_ids=true, to_apply=%region_25.26 | all-reduce | flops 4224 | bytes 33792 | tf_op jit(solution)/shard_map/psum | solution.py:50
  649.6 18.2 %all-reduce.1 = (f32[2048]{0:T(1024)S(1)}, f32[2048]{0:T(1024)S(1)}, f32[64]{0:T(128)S(1)}, f32[64]{0:T(128)S(1)}) all-reduce(f32[2048]{0:T(1024)S(1)} %get-tuple-element.76, f32[2048]{0:T(1024)S(1)} %get-tuple-element.77, f32[64]{0:T(128)S(1)} %get-tuple-element.78, ...), channel_id=1, replica_groups=mesh['dp_0'=4,'dp_1'=2,'seq'=4,'head'=4] {'seq'}, use_global_device_ids=true, to_apply=%region_27.28 | all-reduce | flops 4224 | bytes 33792 | tf_op jit(solution)/shard_map/psum | solution.py:50
  667.9 18.5 %all-reduce = (f32[2048]{0:T(1024)}, f32[2048]{0:T(1024)}, f32[64]{0:T(128)}, f32[64]{0:T(128)}) all-reduce(f32[2048]{0:T(1024)S(1)} %get-tuple-element.68, f32[2048]{0:T(1024)S(1)} %get-tuple-element.69, f32[64]{0:T(128)S(1)} %get-tuple-element.70, ...), channel_id=1, replica_groups=mesh['dp_0'=4,'dp_1'=2,'seq'=4,'head'=4] {'head'}, use_global_device_ids=true, to_apply=%region_28.29 | all-reduce | flops 4224 | bytes 33792 | tf_op jit(solution)/shard_map/psum | solution.py:50
  688.7 641.6 %reduce-scatter.8.cloned.1.call-done = f32[16,4480]{1,0:T(8,128)} async-done(((f32[2048,4480]{1,0:T(8,128)}), f32[16,4480]{1,0:T(8,128)}) %reduce-scatter.8.cloned.1.call-update) | async-done | bytes 286736 | tf_op jit(solution)/shard_map/reduce_scatter | solution.py:282
  (346 shorter events, 139.7 us)
Async XLA Ops:
  7.2 241.0 %copy-start = (bf16[448,2048]{1,0:T(8,128)(2,1)S(1)}, bf16[448,2048]{1,0:T(8,128)(2,1)}, u32[]{:S(2)}) copy-start(bf16[448,2048]{1,0:T(8,128)(2,1)} %param.15) | copy-start | bytes 5505028
  7.2 19.9 %copy-start.85 = (s32[7]{0:T(128)}, s32[7]{0:T(128)S(1)}, u32[]{:S(2)}) copy-start(s32[7]{0:T(128)S(1)} %fusion.195) | copy-start | bytes 88
  26.4 7.9 copy-start.94
  29.9 16.7 %all-to-all-start = ((bf16[2,64,8,384]{3,1,0,2:T(8,128)(2,1)}), bf16[2,64,8,384]{3,1,0,2:T(8,128)(2,1)S(1)}, u32[]{:S(2)}, u32[]{:S(2)}) async-start(bf16[2,64,8,384]{3,1,0,2:T(8,128)(2,1)} %copy.172), calls=%async_computation | async-start | bytes 1572864 | tf_op jit(solution)/shard_map/all_to_all | solution.py:118
  48.8 18.3 %all-to-all-start.1 = ((bf16[4,2,256,2,128]{2,4,3,1,0:T(8,128)(2,1)}), bf16[4,2,256,2,128]{2,4,3,1,0:T(8,128)(2,1)S(1)}, u32[]{:S(2)}, u32[]{:S(2)}) async-start(bf16[4,2,256,2,128]{2,4,3,1,0:T(8,128)(2,1)} %broadcast_in_dim.76), calls=%async_computation.1 | async-start | bytes 2097152 | tf_op jit(solution)/shard_map/all_to_all | solution.py:29
  53.3 122.4 %all-gather.3.cloned.1.call-start = ((), (), s32[]{:S(2)}) async-start(), calls=%async_computation.9 | async-start | bytes 8912896 | tf_op jit(solution)/shard_map/all_gather | solution.py:169
  67.3 12.4 copy-start.28
  68.1 11.6 copy-start.6
  70.6 9.0 copy-start.56
  71.9 7.8 copy-start.58
  82.2 17.7 %copy-start.4 = (bf16[2,64,2048]{2,1,0:T(8,128)(2,1)S(1)}, bf16[2,64,2048]{2,1,0:T(8,128)(2,1)}, u32[]{:S(2)}) copy-start(bf16[2,64,2048]{2,1,0:T(8,128)(2,1)} %param.11) | copy-start | bytes 1572868
  104.4 253.1 %copy-start.82 = (f32[2,64]{1,0:T(2,128)}, f32[2,64]{1,0:T(2,128)S(1)}, u32[]{:S(2)}) copy-start(f32[2,64]{1,0:T(2,128)S(1)} %add_rsqrt_fusion.2) | copy-start | bytes 1540
  106.4 141.8 %all-gather.5.cloned.1.call-start = ((), (), s32[]{:S(2)}) async-start(), calls=%async_computation.11 | async-start | bytes 8912896 | tf_op jit(solution)/shard_map/all_gather | solution.py:192
  107.1 250.4 %reduce-scatter.6.cloned.1.call-start = ((), (), s32[]{:S(2)}) async-start(), calls=%async_computation.12 | async-start | bytes 8912896 | tf_op jit(solution)/shard_map/reduce_scatter | solution.py:203
  248.2 12.7 copy-start.96
  272.7 172.6 %reduce-scatter.4.cloned.1.call-start = ((), (), s32[]{:S(2)}) async-start(), calls=%async_computation.10 | async-start | bytes 8912896 | tf_op jit(solution)/shard_map/reduce_scatter | solution.py:180
  283.7 73.8 %copy-start.15 = (f32[2,64,2048]{2,1,0:T(8,128)S(1)}, f32[2,64,2048]{2,1,0:T(8,128)}, u32[]{:S(2)}) copy-start(f32[2,64,2048]{2,1,0:T(8,128)} %copy-done.14) | copy-start | bytes 3145732
  285.3 160.0 %copy-start.71 = (f32[2048]{0:T(1024)S(1)}, f32[2048]{0:T(1024)}, u32[]{:S(2)}) copy-start(f32[2048]{0:T(1024)} %param.17) | copy-start | bytes 24580
  286.2 159.2 %copy-start.31 = (bf16[2,64,2048]{2,1,0:T(8,128)(2,1)S(1)}, bf16[2,64,2048]{2,1,0:T(8,128)(2,1)}, u32[]{:S(2)}) copy-start(bf16[2,64,2048]{2,1,0:T(8,128)(2,1)} %param.21) | copy-start | bytes 1572868
  455.2 17.1 %all-to-all-start.3 = ((bf16[2,64,8,256]{3,1,0,2:T(8,128)(2,1)}), bf16[2,64,8,256]{3,1,0,2:T(8,128)(2,1)S(1)}, u32[]{:S(2)}, u32[]{:S(2)}) async-start(bf16[2,64,8,256]{3,1,0,2:T(8,128)(2,1)} %copy.188), calls=%async_computation.5 | async-start | bytes 1048576 | tf_op jit(solution)/shard_map/all_to_all | solution.py:221
  494.2 18.5 %all-to-all-start.4 = ((bf16[4,2,256,2,128]{2,4,3,1,0:T(8,128)(2,1)}), bf16[4,2,256,2,128]{2,4,3,1,0:T(8,128)(2,1)}, u32[]{:S(2)}, u32[]{:S(2)}) async-start(bf16[4,2,256,2,128]{2,4,3,1,0:T(8,128)(2,1)} %bitcast.536), calls=%async_computation.6 | async-start | bytes 2097152 | tf_op jit(solution)/shard_map/all_to_all | solution.py:44
  516.0 23.8 %all-to-all-start.5 = ((bf16[2,256,2,384]{3,2,0,1:T(2,128)(2,1)}), bf16[2,256,2,384]{3,2,0,1:T(2,128)(2,1)S(1)}, u32[]{:S(2)}, u32[]{:S(2)}) async-start(bf16[2,256,2,384]{3,2,0,1:T(2,128)(2,1)} %pad_maximum_fusion.6), calls=%async_computation.7 | async-start | bytes 1572864 | tf_op jit(solution)/shard_map/all_to_all | solution.py:258
  520.5 89.9 %all-reduce.7.cloned.1.call-start = ((), (), s32[]{:S(2)}) async-start(), calls=%async_computation.14 | async-start | bytes 11010048 | tf_op jit(solution)/shard_map/psum | solution.py:289
  531.4 799.0 %reduce-scatter.8.cloned.1.call-start = ((), (), s32[]{:S(2)}) async-start(), calls=%async_computation.13 | async-start | bytes 36986880 | tf_op jit(solution)/shard_map/reduce_scatter | solution.py:282
  557.0 7.9 copy-start.17
  562.0 9.1 copy-start.5
  562.0 9.1 copy-start.54
  562.0 9.1 copy-start.73
  571.1 9.2 copy-start.24
  610.3 9.1 copy-start.32
  621.9 9.1 copy-start.80
  621.9 711.6 %copy-start.1 = (bf16[448,2048]{1,0:T(8,128)(2,1)S(1)}, bf16[448,2048]{1,0:T(8,128)(2,1)}, u32[]{:S(2)}) copy-start(bf16[448,2048]{1,0:T(8,128)(2,1)} %param.15) | copy-start | bytes 5505028
  (78 other events, 308.9 us)
Sparse Core Ops, SparseCore 0:
  106.5 69.1 all-gather.2
  177.8 70.3 all-gather.4
  272.8 84.7 reduce-scatter.5
  360.8 84.4 reduce-scatter.3
  531.5 78.8 all-reduce.6
  612.6 717.7 reduce-scatter.7
where the time goes:
time: 1350 us; the launch traced here: 1340 us
  waiting for transfers between devices  954 us (71%)
  matrix products  149 us (11%)
  other arithmetic  68.6 us (5%)
  local copies, waits for them, and re-layouts  66 us (5%)
  blocking collectives  65.8 us (5%)
  starting transfers between devices  22.1 us (2%)
  between operations  15.8 us (1%)
    reduce_scatter x1, waiting for transfers between devices, body(): lax.psum_scatter(jnp.concatenate([left, right], 1), DP_SEQ_HEAD, scatter_...  642 us
    reduce_scatter x1, waiting for transfers between devices, body(): lax.psum_scatter(jnp.einsum('ft,fd->td', part, w_ffn_out, preferred_eleme...  85.5 us
    all_gather x1, waiting for transfers between devices, body(): lax.all_gather(h2.reshape(1, rows * tok, width), ('seq', 'head'), axis=0,...  68.5 us
    reduce_scatter x1, waiting for transfers between devices, body(): lax.psum_scatter(jnp.einsum('fct,fcd->td', part, w_ffn_in, preferred_elem...  65.9 us
    all_gather x1, waiting for transfers between devices, body(): lax.all_gather(d_out.reshape(1, rows * tok, width), ('seq', 'head'), axis...  58.3 us
    psum x4, blocking collectives, one_axis_at_a_time(): array = lax.psum(array, axis)  55.3 us
  transfers between devices with their start and end apart: 11, of which 9 were waited for; matrix products, arithmetic and copies ran while one was open for 12% of the time, Pallas kernels for 0%

commit v1 on v0

v1 whole, which is shorter than its diff:
```python
import functools
import math

import jax
import jax.numpy as jnp
from jax import lax
from jax.experimental import pallas as pl
from jax.experimental.pallas import tpu as pltpu
from jax.sharding import Mesh
from jax.sharding import PartitionSpec as P

HEADS = 28
KV = 7
HD = 64
PER_GROUP = HEADS // KV
DP_SEQ_HEAD = ("dp_0", "dp_1", "seq", "head")
DP = ("dp_0", "dp_1")
RING = 4
BLOCK = 64
MESH = pl.DeviceIdType.MESH
EPS = 1e-06
SCALE = 0.125
f32 = jnp.float32
bf16 = jnp.bfloat16
VMEM_BYTES = 60 * 2**20


def nt(a, b):
    return lax.dot_general(a, b, (((1,), (1,)), ((), ())), preferred_element_type=f32)


def nn(a, b):
    return lax.dot_general(a, b, (((1,), (0,)), ((), ())), preferred_element_type=f32)


def tn(a, b):
    return lax.dot_general(a, b, (((0,), (0,)), ((), ())), preferred_element_type=f32)


def shift(index, by):
    return lax.rem(index + (by + RING), RING)


def barrier_with(axes):
    barrier = pltpu.get_barrier_semaphore()
    for axis in axes:
        index = lax.axis_index(axis)
        for by in (1, -1):
            pl.semaphore_signal(
                barrier, inc=1, device_id={axis: shift(index, by)}, device_id_type=MESH
            )
    pl.semaphore_wait(barrier, 2 * len(axes))


class Copies:
    def __init__(self, send, recv):
        self.send = send
        self.recv = recv
        self.started = []

    def start(self, slot, src, dst, axis, by):
        copy = pltpu.make_async_remote_copy(
            src_ref=src,
            dst_ref=dst,
            send_sem=self.send.at[slot],
            recv_sem=self.recv.at[slot],
            device_id={axis: shift(lax.axis_index(axis), by)},
            device_id_type=MESH,
        )
        copy.start()
        self.started.append(copy)
        return copy

    def finish(self):
        for copy in self.started:
            copy.wait_send()


INNER = ("head", "seq")
GROUP = ("seq", "head")


class PlaneGather:
    def __init__(self, copies, base, half, own, buf):
        self.c = copies
        self.base = base + 8 * half
        self.half = half
        self.own = own
        self.buf = buf
        self.i = lax.axis_index(INNER[half])
        self.g = lax.axis_index(GROUP[half])

    def row(self, by=0):
        return 4 * self.half + shift(self.g, by)

    def step1(self):
        ax = INNER[self.half]
        dst = self.buf.at[self.row(), self.i]
        self.a = self.c.start(self.base, self.own, dst, ax, 1)
        self.b = self.c.start(self.base + 1, self.own, dst, ax, -1)

    def step2(self):
        ax = INNER[self.half]
        n = self.buf.shape[2] // 2
        self.a.wait_recv()
        left = self.buf.at[self.row(), shift(self.i, -1), pl.ds(0, n)]
        self.a = self.c.start(self.base + 2, left, left, ax, 1)
        self.b.wait_recv()
        right = self.buf.at[self.row(), shift(self.i, 1), pl.ds(n, n)]
        self.b = self.c.start(self.base + 3, right, right, ax, -1)

    def step3(self):
        ax = GROUP[self.half]
        self.a.wait_recv()
        self.b.wait_recv()
        rows = self.buf.at[self.row()]
        self.a = self.c.start(self.base + 4, rows, rows, ax, 1)
        self.b = self.c.start(self.base + 5, rows, rows, ax, -1)

    def step4(self):
        ax = GROUP[self.half]
        self.a.wait_recv()
        left = self.buf.at[self.row(-1), pl.ds(0, 2)]
        self.a = self.c.start(self.base + 6, left, left, ax, 1)
        self.b.wait_recv()
        right = self.buf.at[self.row(1), pl.ds(2, 2)]
        self.b = self.c.start(self.base + 7, right, right, ax, -1)

    def finish(self):
        self.a.wait_recv()
        self.b.wait_recv()


class PlaneSum:
    def __init__(self, copies, base, half, part, land1, land2, land3, land4):
        self.c = copies
        self.base = base + 8 * half
        self.half = half
        self.part = part
        self.l1, self.l2, self.l3, self.l4 = (
            ref.at[half] for ref in (land1, land2, land3, land4)
        )
        self.i = lax.axis_index(INNER[half])
        self.g = lax.axis_index(GROUP[half])

    def row(self, by=0):
        return 4 * self.half + shift(self.g, by)

    def add(self, ref, other):
        ref[...] = (ref[...].astype(f32) + other[...].astype(f32)).astype(ref.dtype)

    def step1(self):
        ax = GROUP[self.half]
        row = self.row(2)
        self.a = self.c.start(self.base, self.part.at[row, pl.ds(0, 2)], self.l1.at[0], ax, 1)
        self.b = self.c.start(self.base + 1, self.part.at[row, pl.ds(2, 2)], self.l1.at[1], ax, -1)

    def step2(self):
        ax = GROUP[self.half]
        self.a.wait_recv()
        self.add(self.part.at[self.row(1), pl.ds(0, 2)], self.l1.at[0])
        self.a = self.c.start(self.base + 2, self.part.at[self.row(1)], self.l2.at[0], ax, 1)
        self.b.wait_recv()
        self.add(self.part.at[self.row(-1), pl.ds(2, 2)], self.l1.at[1])
        self.b = self.c.start(self.base + 3, self.part.at[self.row(-1)], self.l2.at[1], ax, -1)

    def step3(self):
        ax = INNER[self.half]
        n = self.part.shape[2] // 2
        self.a.wait_recv()
        self.b.wait_recv()
        rows = self.part.at[self.row()]
        rows[...] = (
            rows[...].astype(f32) + self.l2[0].astype(f32) + self.l2[1].astype(f32)
        ).astype(rows.dtype)
        block = self.part.at[self.row(), shift(self.i, 2)]
        self.a = self.c.start(self.base + 4, block.at[pl.ds(0, n)], self.l3.at[0], ax, 1)
        self.b = self.c.start(self.base + 5, block.at[pl.ds(n, n)], self.l3.at[1], ax, -1)

    def step4(self):
        ax = INNER[self.half]
        n = self.part.shape[2] // 2
        self.a.wait_recv()
        right = self.part.at[self.row(), shift(self.i, 1)]
        self.add(right.at[pl.ds(0, n)], self.l3.at[0])
        self.a = self.c.start(self.base + 6, right, self.l4.at[0], ax, 1)
        self.b.wait_recv()
        left = self.part.at[self.row(), shift(self.i, -1)]
        self.add(left.at[pl.ds(n, n)], self.l3.at[1])
        self.b = self.c.start(self.base + 7, left, self.l4.at[1], ax, -1)

    def result(self):
        self.a.wait_recv()
        self.b.wait_recv()
        own = self.part[self.row(), self.i].astype(f32)
        return own + self.l4[0].astype(f32) + self.l4[1].astype(f32)


def sum_landings(columns):
    return [
        pltpu.VMEM((2, 2, 2, BLOCK, columns), bf16),
        pltpu.VMEM((2, 2, 4, BLOCK, columns), bf16),
        pltpu.VMEM((2, 2, BLOCK // 2, columns), bf16),
        pltpu.VMEM((2, 2, BLOCK, columns), bf16),
    ]


def ffn_kernel(
    h2_ref,
    dy_ref,
    win_ref,
    wdn_ref,
    outp_ref,
    dh2_ref,
    gin_ref,
    gdn_ref,
    h2a,
    dya,
    win,
    wdn,
    hid,
    dbo,
    dpt,
    l1,
    l2,
    l3,
    l4,
    stage,
    gstage,
    send,
    recv,
    lsem,
    osem,
    gsem,
):
    units = wdn.shape[0]
    width = wdn.shape[1]
    copies = Copies(send, recv)
    weights = [
        pltpu.make_async_copy(win_ref, win, lsem.at[8]),
        pltpu.make_async_copy(wdn_ref, wdn, lsem.at[9]),
    ]
    for copy in weights:
        copy.start()
    loads = []
    for j in range(4):
        loads.append(pltpu.make_async_copy(dy_ref.at[j, :, 0], dya.at[j], lsem.at[j]))
        loads.append(pltpu.make_async_copy(dy_ref.at[:, j, 1], dya.at[4 + j], lsem.at[4 + j]))
    for copy in loads:
        copy.start()
    barrier_with(("seq", "head"))
    gathers = [PlaneGather(copies, 0, half, h2_ref.at[half], h2a) for half in (0, 1)]
    for gather in gathers:
        gather.step1()
    for half in (0, 1):
        h2a[gathers[half].row(), gathers[half].i] = h2_ref[half]
    for gather in gathers:
        gather.step2()
    for copy in weights + loads:
        copy.wait()
    for gather in gathers:
        gather.step3()
    seq, head = lax.axis_index("seq"), lax.axis_index("head")

    def group(half, by):
        return 4 * half + lax.rem(seq + half * (head - seq) + by + 4, 4)

    def rows_of(ref, q):
        return ref[q].reshape(4 * BLOCK, width)

    def columns_of(q):
        return pl.ds(pl.multiple_of(q * 4 * BLOCK, 4 * BLOCK), 4 * BLOCK)

    def forward(q):
        both = nt(win[...], rows_of(h2a, q))
        d_hidden = nt(wdn[...], rows_of(dya, q))
        gate = both[:units]
        up = both[units:]
        sig = 1.0 / (1.0 + jnp.exp(-gate))
        act = gate * sig
        cols = columns_of(q)
        hid[:, cols] = (act * up).astype(bf16)
        dbo[:units, cols] = (d_hidden * up * (sig * (1.0 + gate * (1.0 - sig)))).astype(bf16)
        dbo[units:, cols] = (d_hidden * act).astype(bf16)

    def back(q):
        value = tn(dbo[:, columns_of(q)], win[...])
        dpt[q] = value.astype(bf16).reshape(4, BLOCK, width)

    @pl.loop(0, 2)
    def _(half):
        forward(group(half, 0))

    for gather in gathers:
        gather.step4()

    @pl.loop(0, 4)
    def _(k):
        forward(group(lax.div(k, 2), 1 - 2 * lax.rem(k, 2)))

    for gather in gathers:
        gather.finish()

    @pl.loop(0, 2)
    def _(half):
        forward(group(half, 2))
        back(group(half, 2))

    sums = [PlaneSum(copies, 16, half, dpt, l1, l2, l3, l4) for half in (0, 1)]
    for total in sums:
        total.step1()

    @pl.loop(0, 4)
    def _(k):
        back(group(lax.div(k, 2), 1 - 2 * lax.rem(k, 2)))

    for total in sums:
        total.step2()

    @pl.loop(0, 2)
    def _(half):
        back(group(half, 0))

    tile = gstage.shape[2]
    tiles = width // tile
    tokens = 8 * 4 * BLOCK
    gcopies = []
    for n in range(tiles):
        cols = pl.ds(n * tile, tile)
        if n >= 2:
            for copy in gcopies[n - 2]:
                copy.wait()
        slot = n % 2
        gstage[slot, : 2 * units] = nn(
            dbo[...], h2a[:, :, :, cols].reshape(tokens, tile)
        ).astype(bf16)
        gstage[slot, 2 * units :] = nn(
            hid[...], dya[:, :, :, cols].reshape(tokens, tile)
        ).astype(bf16)
        pair = [
            pltpu.make_async_copy(
                gstage.at[slot, pl.ds(0, 2 * units)], gin_ref.at[:, cols], gsem.at[slot, 0]
            ),
            pltpu.make_async_copy(
                gstage.at[slot, pl.ds(2 * units, units)], gdn_ref.at[:, cols], gsem.at[slot, 1]
            ),
        ]
        for copy in pair:
            copy.start()
        gcopies.append(pair)
    for total in sums:
        total.step3()
    for pair in gcopies[-2:]:
        for copy in pair:
            copy.wait()

    def out_copy(q):
        slot = q % 2
        place = outp_ref.at[q, :, 0] if q < 4 else outp_ref.at[:, q - 4, 1]
        return pltpu.make_async_copy(stage.at[slot], place, osem.at[slot])

    def out_part(q):
        if q >= 2:
            out_copy(q - 2).wait()
        value = tn(hid[:, pl.ds(q * 4 * BLOCK, 4 * BLOCK)], wdn[...])
        stage[q % 2] = value.astype(bf16).reshape(4, BLOCK, width)
        out_copy(q).start()

    for q in range(4):
        out_part(q)
    for total in sums:
        total.step4()
    for q in range(4, 8):
        out_part(q)
    for half in (0, 1):
        dh2_ref[half] = sums[half].result()
    out_copy(6).wait()
    out_copy(7).wait()
    copies.finish()


def ffn(h2, dy_all, w_in, w_down):
    units, width = w_down.shape
    tokens = 32 * BLOCK
    tile = 512
    any_spec = pl.BlockSpec(memory_space=pl.ANY)
    vmem_spec = pl.BlockSpec(memory_space=pltpu.VMEM)
    return pl.pallas_call(
        ffn_kernel,
        out_shape=(
            jax.ShapeDtypeStruct((4, 4, 2, BLOCK, width), bf16),
            jax.ShapeDtypeStruct((2, BLOCK, width), f32),
            jax.ShapeDtypeStruct((2 * units, width), bf16),
            jax.ShapeDtypeStruct((units, width), bf16),
        ),
        in_specs=[vmem_spec, any_spec, any_spec, any_spec],
        out_specs=(any_spec, vmem_spec, any_spec, any_spec),
        scratch_shapes=[
            pltpu.VMEM((8, 4, BLOCK, width), bf16),
            pltpu.VMEM((8, 4, BLOCK, width), bf16),
            pltpu.VMEM((2 * units, width), bf16),
            pltpu.VMEM((units, width), bf16),
            pltpu.VMEM((units, tokens), bf16),
            pltpu.VMEM((2 * units, tokens), bf16),
            pltpu.VMEM((8, 4, BLOCK, width), bf16),
            *sum_landings(width),
            pltpu.VMEM((2, 4, BLOCK, width), bf16),
            pltpu.VMEM((2, 3 * units, tile), bf16),
            pltpu.SemaphoreType.DMA((32,)),
            pltpu.SemaphoreType.DMA((32,)),
            pltpu.SemaphoreType.DMA((10,)),
            pltpu.SemaphoreType.DMA((2,)),
            pltpu.SemaphoreType.DMA((2, 2)),
        ],
        compiler_params=pltpu.CompilerParams(
            collective_id=1, has_side_effects=True, vmem_limit_bytes=VMEM_BYTES
        ),
        name="ffn",
    )(h2, dy_all, w_in, w_down)


def mask_rows(starts_ref, row, transposed, mask_ref):
    seq, head = lax.axis_index("seq"), lax.axis_index("head")
    keys = 16 * BLOCK
    index = lax.broadcasted_iota(jnp.int32, (1, keys), 1)
    if transposed:
        group = lax.div(index, 4 * BLOCK)
        inner = lax.rem(lax.div(index, BLOCK), 4)
        k_pos = (inner * 4 + group) * BLOCK + lax.rem(index, BLOCK)
    else:
        k_pos = index
    first = (seq * 4 + head) * BLOCK
    q_pos = first + lax.broadcasted_iota(jnp.int32, (BLOCK, 1), 0)
    k_doc = jnp.zeros((1, keys), jnp.int32)
    q_doc = jnp.zeros((BLOCK, 1), jnp.int32)
    for d in range(starts_ref.shape[1]):
        start = starts_ref[row, d]
        k_doc += (start <= k_pos).astype(jnp.int32)
        q_doc += (start <= q_pos).astype(jnp.int32)
    seen = (k_pos <= q_pos) & (k_doc == q_doc)
    mask_ref[row] = seen.astype(f32)


LOG2E_SCALE = SCALE * math.log2(math.e)


def stacked(block, where):
    rows = jnp.concatenate([block[:, h * HD : (h + 1) * HD] for h in range(PER_GROUP)], 0)
    zero = jnp.zeros_like(rows)
    return jnp.concatenate([rows, zero] if where == 0 else [zero, rows], 1)


def unstacked(rows):
    return jnp.concatenate([rows[h * BLOCK : (h + 1) * BLOCK] for h in range(PER_GROUP)], 1)


def weights_of(q_rows, kv_rows, mask):
    scores = nt(q_rows, kv_rows)
    keys = kv_rows.shape[0]
    e = jnp.exp2(scores * LOG2E_SCALE).reshape(PER_GROUP, BLOCK, keys) * mask[None]
    return e.reshape(PER_GROUP * BLOCK, keys)


def attend_kernel(starts_ref, q_ref, kv_ref, o_ref, kva_ref, kva, mask, send, recv, lsem):
    copies = Copies(send, recv)
    barrier_with(("seq", "head"))
    gathers = [PlaneGather(copies, 0, half, kv_ref.at[half], kva) for half in (0, 1)]
    for gather in gathers:
        gather.step1()
    for half in (0, 1):
        kva[gathers[half].row(), gathers[half].i] = kv_ref[half]
    mask_rows(starts_ref, 0, False, mask)
    mask_rows(starts_ref, 1, True, mask)
    for gather in gathers:
        gather.step2()
    for gather in gathers:
        gather.step3()
    for gather in gathers:
        gather.step4()
    for gather in gathers:
        gather.finish()
    keep = pltpu.make_async_copy(kva, kva_ref, lsem)
    keep.start()

    @pl.loop(0, 2)
    def _(row):
        for g in range(KV):
            rows = pl.ds(pl.multiple_of(row * BLOCK, BLOCK), BLOCK)
            cols = slice(g * PER_GROUP * HD, (g + 1) * PER_GROUP * HD)
            q_rows = stacked(q_ref[rows, cols], 0)
            kv_rows = kva[pl.ds(row * 4, 4), :, :, g * 2 * HD : (g + 1) * 2 * HD].reshape(
                16 * BLOCK, 2 * HD
            )
            e = weights_of(q_rows, kv_rows, mask[row])
            total = jnp.sum(e, axis=1, keepdims=True)
            mixed = nn(e.astype(bf16), kv_rows)[:, HD:] / total
            o_ref[rows, cols] = unstacked(mixed.astype(bf16))

    keep.wait()
    copies.finish()


def attend(starts, q, kv):
    vmem_spec = pl.BlockSpec(memory_space=pltpu.VMEM)
    return pl.pallas_call(
        attend_kernel,
        out_shape=(
            jax.ShapeDtypeStruct(q.shape, bf16),
            jax.ShapeDtypeStruct((8, 4, BLOCK, kv.shape[2]), bf16),
        ),
        in_specs=[pl.BlockSpec(memory_space=pltpu.SMEM), vmem_spec, vmem_spec],
        out_specs=(vmem_spec, pl.BlockSpec(memory_space=pl.ANY)),
        scratch_shapes=[
            pltpu.VMEM((8, 4, BLOCK, kv.shape[2]), bf16),
            pltpu.VMEM((2, BLOCK, 16 * BLOCK), f32),
            pltpu.SemaphoreType.DMA((16,)),
            pltpu.SemaphoreType.DMA((16,)),
            pltpu.SemaphoreType.DMA,
        ],
        compiler_params=pltpu.CompilerParams(
            collective_id=2, has_side_effects=True, vmem_limit_bytes=VMEM_BYTES
        ),
        name="attend",
    )(starts, q, kv)


def attend_back_kernel(
    starts_ref, q_ref, do_ref, kva_ref, dq_ref, dkv_ref, kva, part, mask, l1, l2, l3, l4, send, recv, lsem
):
    copies = Copies(send, recv)
    load = pltpu.make_async_copy(kva_ref, kva, lsem)
    load.start()
    barrier_with(("seq", "head"))
    mask_rows(starts_ref, 0, False, mask)
    mask_rows(starts_ref, 1, True, mask)
    load.wait()
    sums = [PlaneSum(copies, 0, half, part, l1, l2, l3, l4) for half in (0, 1)]

    @pl.loop(0, 2)
    def _(row):
        for g in range(KV):
            rows = pl.ds(pl.multiple_of(row * BLOCK, BLOCK), BLOCK)
            cols = slice(g * PER_GROUP * HD, (g + 1) * PER_GROUP * HD)
            lanes = slice(g * 2 * HD, (g + 1) * 2 * HD)
            q_rows = stacked(q_ref[rows, cols], 0)
            do_rows = stacked(do_ref[rows, cols], 1)
            kv_rows = kva[pl.ds(row * 4, 4), :, :, lanes].reshape(16 * BLOCK, 2 * HD)
            e = weights_of(q_rows, kv_rows, mask[row])
            probs = e * (1.0 / jnp.sum(e, axis=1, keepdims=True))
            d_probs = nt(do_rows, kv_rows)
            delta = jnp.sum(probs * d_probs, axis=1, keepdims=True)
            d_scores = (probs * (d_probs - delta)).astype(bf16)
            dq = nn(d_scores, kv_rows)[:, :HD] * SCALE
            dq_ref[rows, cols] = unstacked(dq.astype(bf16))
            dkv = tn(d_scores, q_rows * jnp.asarray(SCALE, bf16)) + tn(probs.astype(bf16), do_rows)
            part[pl.ds(row * 4, 4), :, :, lanes] = dkv.astype(bf16).reshape(4, 4, BLOCK, 2 * HD)

    for total in sums:
        total.step1()
    for total in sums:
        total.step2()
    for total in sums:
        total.step3()
    for total in sums:
        total.step4()
    for half in (0, 1):
        dkv_ref[half] = sums[half].result().astype(bf16)
    copies.finish()


def attend_back(starts, q, d_o, kva):
    vmem_spec = pl.BlockSpec(memory_space=pltpu.VMEM)
    columns = kva.shape[3]
    return pl.pallas_call(
        attend_back_kernel,
        out_shape=(
            jax.ShapeDtypeStruct(q.shape, bf16),
            jax.ShapeDtypeStruct((2, BLOCK, columns), bf16),
        ),
        in_specs=[
            pl.BlockSpec(memory_space=pltpu.SMEM),
            vmem_spec,
            vmem_spec,
            pl.BlockSpec(memory_space=pl.ANY),
        ],
        out_specs=(vmem_spec, vmem_spec),
        scratch_shapes=[
            pltpu.VMEM((8, 4, BLOCK, columns), bf16),
            pltpu.VMEM((8, 4, BLOCK, columns), bf16),
            pltpu.VMEM((2, BLOCK, 16 * BLOCK), f32),
            *sum_landings(columns),
            pltpu.SemaphoreType.DMA((16,)),
            pltpu.SemaphoreType.DMA((16,)),
            pltpu.SemaphoreType.DMA,
        ],
        compiler_params=pltpu.CompilerParams(
            collective_id=3, has_side_effects=True, vmem_limit_bytes=VMEM_BYTES
        ),
        name="attend_back",
    )(starts, q, d_o, kva)


AXIS_ORDERS = (("dp_0", "seq", "head"), ("seq", "head", "dp_0"), ("head", "dp_0", "seq"))
CHIP_AXES = ("dp_0", "seq", "head")


class RingSum:
    def __init__(self, copies, base, axis, part, half_land, full_land):
        self.c = copies
        self.base = base
        self.axis = axis
        self.part = part
        self.hl = half_land
        self.fl = full_land
        self.i = lax.axis_index(axis)

    def step1(self):
        far = self.part.at[shift(self.i, 2)]
        self.a = self.c.start(self.base, far.at[pl.ds(0, 2)], self.hl.at[0], self.axis, 1)
        self.b = self.c.start(self.base + 1, far.at[pl.ds(2, 2)], self.hl.at[1], self.axis, -1)

    def step2(self):
        for copy, by, side in ((self.a, 1, 0), (self.b, -1, 1)):
            copy.wait_recv()
            block = self.part.at[shift(self.i, by)]
            half = block.at[pl.ds(2 * side, 2)]
            half[...] = (half[...].astype(f32) + self.hl[side].astype(f32)).astype(bf16)
            new = self.c.start(self.base + 2 + side, block, self.fl.at[side], self.axis, by)
            if side == 0:
                self.a = new
            else:
                self.b = new

    def finish(self):
        self.a.wait_recv()
        self.b.wait_recv()
        own = self.part.at[self.i]
        own[...] = (
            own[...].astype(f32) + self.fl[0].astype(f32) + self.fl[1].astype(f32)
        ).astype(bf16)
        return own


def projections_kernel(
    h1_ref, da_ref, dqkv_ref, mix_ref, gain_ref, out_ref, gain_out, *scratch
):
    (h1c, dac, dqc, mxc, gsum) = scratch[:5]
    parts = scratch[5:8]
    half1, full1, half2, full2, last = (scratch[8 + 3 * k : 11 + 3 * k] for k in range(5))
    send, recv = scratch[23:]
    tokens = h1_ref.shape[0]
    copies = Copies(send, recv)
    barrier = pltpu.get_barrier_semaphore()
    core = lax.axis_index("dp_1")
    other = 1 - core
    for axis in CHIP_AXES:
        for by in (1, 2, 3):
            pl.semaphore_signal(
                barrier,
                inc=1,
                device_id={axis: shift(lax.axis_index(axis), by)},
                device_id_type=MESH,
            )
    pl.semaphore_signal(barrier, inc=1, device_id={"dp_1": other}, device_id_type=MESH)
    pl.semaphore_wait(barrier, 10)

    def to_other(slot, src, dst):
        copy = pltpu.make_async_remote_copy(
            src_ref=src,
            dst_ref=dst,
            send_sem=send.at[slot],
            recv_sem=recv.at[slot],
            device_id={"dp_1": other},
            device_id_type=MESH,
        )
        copy.start()
        copies.started.append(copy)
        return copy

    mine, theirs = pl.ds(0, tokens), pl.ds(tokens, tokens)

    def piece(z, which):
        return pl.ds(pl.multiple_of(z * 512 + which * 256, 256), 256)

    moves = [
        to_other(0, dqkv_ref, dqc.at[theirs]),
        to_other(1, mix_ref, mxc.at[theirs]),
    ]
    for z in range(4):
        cols = pl.ds(z * 256, 256)
        moves.append(to_other(2 + 2 * z, h1_ref.at[:, piece(z, other)], h1c.at[theirs, cols]))
        moves.append(to_other(3 + 2 * z, da_ref.at[:, piece(z, other)], dac.at[theirs, cols]))
    gain_move = to_other(10, gain_ref, gsum.at[3, core])
    for z in range(4):
        cols = pl.ds(z * 256, 256)
        h1c[mine, cols] = h1_ref[:, piece(z, core)]
        dac[mine, cols] = da_ref[:, piece(z, core)]
    dqc[mine] = dqkv_ref[...]
    mxc[mine] = mix_ref[...]
    for move in moves:
        move.wait_recv()

    widths = [part.shape[4] for part in parts]
    split = dqkv_ref.shape[1] - widths[0]
    sources = (
        ((h1c, dqc, 0, widths[0], 0),),
        ((h1c, dqc, widths[0], split, 0), (dac, mxc, 0, widths[1] - split, split)),
        ((dac, mxc, widths[1] - split, widths[2], 0),),
    )

    @pl.loop(0, 4)
    def _(z):
        cols = pl.ds(pl.multiple_of(z * 256, 256), 256)
        for k in range(3):
            for lhs, rhs, first, width, place in sources[k]:
                value = tn(lhs[:, cols], rhs[:, first : first + width]).astype(bf16)
                value = value.reshape(4, 4, 16, width)
                to = slice(place, place + width)
                if k == 0:
                    parts[0][z, :, :, :, to] = value
                elif k == 1:
                    parts[1][:, :, z, :, to] = value
                else:
                    for y in range(4):
                        parts[2][:, z, y, :, to] = value[y]

    def gain_step(k, axis, value):
        i = lax.axis_index(axis)
        gsum[k, i] = value
        out = []
        for n, by in enumerate((1, 2, 3)):
            src = gsum.at[k, i]
            out.append(copies.start(11 + 3 * k + n, src, src, axis, by))
        return out

    def gain_total(k, moves):
        for move in moves:
            move.wait_recv()
        return gsum[k, 0] + gsum[k, 1] + gsum[k, 2] + gsum[k, 3]

    base = 20
    rings = [
        RingSum(copies, base + 4 * k, AXIS_ORDERS[k][0], parts[k], half1[k], full1[k])
        for k in range(3)
    ]
    for ring in rings:
        ring.step1()
    gain_move.wait_recv()
    gsum[3, core] = gain_ref[...]
    total = gsum[3, 0] + gsum[3, 1]
    gmoves = gain_step(0, CHIP_AXES[0], total)
    for ring in rings:
        ring.step2()
    gmoves = gain_step(1, CHIP_AXES[1], gain_total(0, gmoves))
    owns = [ring.finish() for ring in rings]
    rings = [
        RingSum(copies, base + 12 + 4 * k, AXIS_ORDERS[k][1], owns[k], half2[k], full2[k])
        for k in range(3)
    ]
    for ring in rings:
        ring.step1()
    gmoves = gain_step(2, CHIP_AXES[2], gain_total(1, gmoves))
    for ring in rings:
        ring.step2()
    gain_out[...] = gain_total(2, gmoves)
    owns = [ring.finish() for ring in rings]
    ends = []
    for k in range(3):
        axis = AXIS_ORDERS[k][2]
        i = lax.axis_index(axis)
        for n, by in enumerate((1, 2, 3)):
            ends.append(
                copies.start(
                    base + 24 + 3 * k + n, owns[k].at[shift(i, by)], last[k].at[n], axis, by
                )
            )
    for end in ends:
        end.wait_recv()
    place = 0
    for k in range(3):
        i = lax.axis_index(AXIS_ORDERS[k][2])
        value = owns[k][i].astype(f32)
        for n in range(3):
            value = value + last[k][n].astype(f32)
        out_ref[:, place : place + widths[k]] = value
        place += widths[k]
    copies.finish()


def projections(h1, d_attn, d_qkv, mixed, gains):
    tokens, qkv_width = d_qkv.shape
    columns = qkv_width + mixed.shape[1]
    widths = (1536, 1536, columns - 3072)
    vmem_spec = pl.BlockSpec(memory_space=pltpu.VMEM)
    rows = h1.shape[1] // 2

    def each(make):
        return [pltpu.VMEM(make(width), bf16) for width in widths]

    return pl.pallas_call(
        projections_kernel,
        out_shape=(
            jax.ShapeDtypeStruct((16, columns), f32),
            jax.ShapeDtypeStruct(gains.shape, f32),
        ),
        in_specs=[vmem_spec] * 5,
        out_specs=(vmem_spec, vmem_spec),
        scratch_shapes=[
            pltpu.VMEM((2 * tokens, rows), bf16),
            pltpu.VMEM((2 * tokens, rows), bf16),
            pltpu.VMEM((2 * tokens, qkv_width), bf16),
            pltpu.VMEM((2 * tokens, mixed.shape[1]), bf16),
            pltpu.VMEM((4, 4, *gains.shape), f32),
            *each(lambda w: (4, 4, 4, 16, w)),
            *each(lambda w: (2, 2, 4, 16, w)),
            *each(lambda w: (2, 4, 4, 16, w)),
            *each(lambda w: (2, 2, 16, w)),
            *each(lambda w: (2, 4, 16, w)),
            *each(lambda w: (3, 16, w)),
            pltpu.SemaphoreType.DMA((53,)),
            pltpu.SemaphoreType.DMA((53,)),
        ],
        compiler_params=pltpu.CompilerParams(
            collective_id=4, has_side_effects=True, vmem_limit_bytes=VMEM_BYTES
        ),
        name="projections",
    )(h1, d_attn, d_qkv, mixed, gains)


def rms_parts(v):
    inverse = lax.rsqrt(jnp.mean(v * v, axis=-1, keepdims=True) + EPS)
    return (v * inverse, inverse)


def rms_back(grad, normed, inverse):
    return inverse * (grad - normed * jnp.mean(grad * normed, axis=-1, keepdims=True))


def rotate(v, cosine, sine):
    half = v.shape[-1] // 2
    first = v[..., :half]
    second = v[..., half:]
    return jnp.concatenate([first * cosine - second * sine, second * cosine + first * sine], -1)


def angle_tables(positions, width):
    half = width // 2
    freq = jnp.exp(jnp.arange(half, dtype=f32) * (-2.0 * math.log(10000.0) / width))
    angle = positions.astype(f32)[:, None] * freq[None, :]
    return (jnp.cos(angle), jnp.sin(angle))


def body(
    tokens, w_qkv, w_out, w_ffn_in, w_ffn_out, g_attn, g_ffn, q_gain, k_gain, doc_starts, d_out
):
    rows, tok, width = tokens.shape
    count = rows * tok
    n_seq = lax.axis_size("seq")
    n_head = lax.axis_size("head")
    span = tok * n_head
    seq_index = lax.axis_index("seq")
    head_index = lax.axis_index("head")
    tok_pos = seq_index * span + head_index * tok + jnp.arange(tok)
    cosine, sine = angle_tables(tok_pos, HD)
    cosine = cosine[None, :, None, :]
    sine = sine[None, :, None, :]
    dy_all = lax.all_gather(d_out[None], ("seq", "head"), axis=0, tiled=True)
    dy_all = dy_all.reshape(n_seq, n_head, rows, tok, width)
    w_in = w_ffn_in.transpose(1, 0, 2).reshape(-1, width)
    xf = tokens.reshape(count, width).astype(f32)
    dy = d_out.reshape(count, width).astype(f32)
    n1, inv1 = rms_parts(xf)
    h1 = (n1 * g_attn).astype(bf16)
    qkv = jnp.dot(h1, w_qkv, preferred_element_type=f32)
    q_raw = qkv[..., : HEADS * HD].reshape(rows, tok, HEADS, HD)
    k_raw = qkv[..., HEADS * HD : (HEADS + KV) * HD].reshape(rows, tok, KV, HD)
    v_raw = qkv[..., (HEADS + KV) * HD :].reshape(rows, tok, KV, HD)
    q_normed, inv_q = rms_parts(q_raw)
    k_normed, inv_k = rms_parts(k_raw)
    q_rot = rotate(q_normed * q_gain, cosine, sine).astype(bf16).reshape(count, HEADS * HD)
    k_rot = rotate(k_normed * k_gain, cosine, sine)
    kv = jnp.concatenate([k_rot, v_raw], -1).astype(bf16).reshape(rows, tok, KV * 2 * HD)
    mixed, kva = attend(doc_starts, q_rot, kv)
    attn = jnp.dot(mixed, w_out, preferred_element_type=f32)
    r1 = xf + attn
    n2, inv2 = rms_parts(r1)
    h2 = (n2 * g_ffn).astype(bf16)
    outp, d_h2, grad_in, grad_down = ffn(h2.reshape(rows, tok, width), dy_all, w_in, w_ffn_out)
    d_h2 = d_h2.reshape(count, width)
    ffn_sum = lax.psum_scatter(
        outp.reshape(n_seq * n_head * count, width), ("seq", "head"), scatter_dimension=0, tiled=True
    )
    grad_in_sum, grad_down_sum = (
        lax.psum(grad_in, DP).astype(f32),
        lax.psum(grad_down, DP).astype(f32),
    )
    grad_in_sum = grad_in_sum.reshape(2, -1, width).transpose(1, 0, 2)
    grad_gffn = jnp.sum(d_h2 * n2, axis=0)
    d_r1 = dy + rms_back(d_h2 * g_ffn, n2, inv2)
    d_attn = d_r1.astype(bf16)
    d_o = lax.dot_general(
        d_attn, w_out, (((1,), (1,)), ((), ())), preferred_element_type=f32
    ).astype(bf16)
    d_q, d_kv = attend_back(doc_starts, q_rot, d_o, kva)
    d_qrot = d_q.reshape(rows, tok, HEADS, HD).astype(f32)
    d_kv = d_kv.reshape(rows, tok, KV, 2 * HD)
    d_krot = d_kv[..., :HD].astype(f32)
    d_vraw = d_kv[..., HD:]
    d_qs = rotate(d_qrot, cosine, -sine)
    d_ks = rotate(d_krot, cosine, -sine)
    grad_qgain = jnp.sum(d_qs * q_normed, axis=(0, 1, 2))
    grad_kgain = jnp.sum(d_ks * k_normed, axis=(0, 1, 2))
    d_qraw = rms_back(d_qs * q_gain, q_normed, inv_q)
    d_kraw = rms_back(d_ks * k_gain, k_normed, inv_k)
    d_qkv = jnp.concatenate(
        [
            d_qraw.astype(bf16).reshape(count, HEADS * HD),
            d_kraw.astype(bf16).reshape(count, KV * HD),
            d_vraw.reshape(count, KV * HD),
        ],
        -1,
    )
    d_h1 = lax.dot_general(
        d_qkv, w_qkv, (((1,), (1,)), ((), ())), preferred_element_type=f32
    )
    grad_gattn = jnp.sum(d_h1 * n1, axis=0)
    grad_x = (d_r1 + rms_back(d_h1 * g_attn, n1, inv1)).astype(bf16)
    gains = jnp.concatenate([grad_gattn, grad_gffn, grad_qgain, grad_kgain])
    gains = jnp.pad(gains, (0, 40 * 128 - gains.shape[0])).reshape(40, 128)
    weight_part, gains = projections(h1, d_attn, d_qkv, mixed, gains)
    gains = gains.reshape(-1)
    output = (r1 + ffn_sum.astype(f32)).astype(bf16)
    qkv_width = w_qkv.shape[1]
    return (
        output.reshape(rows, tok, width),
        grad_x.reshape(rows, tok, width),
        weight_part[:, :qkv_width],
        weight_part[:, qkv_width:].T,
        grad_in_sum,
        grad_down_sum,
        gains[:width],
        gains[width : 2 * width],
        gains[2 * width : 2 * width + HD],
        gains[2 * width + HD : 2 * width + 2 * HD],
    )


def solution(mesh):
    split = Mesh(
        mesh.devices.reshape(4, 2, mesh.shape["seq"], mesh.shape["head"]),
        ("dp_0", "dp_1", "seq", "head"),
    )
    return jax.shard_map(
        body,
        mesh=split,
        in_specs=(
            P(DP, ("seq", "head"), None),
            P(),
            P(),
            P(("seq", "head"), None, None),
            P(("seq", "head"), None),
            P(),
            P(),
            P(),
            P(),
            P(DP, None),
            P(DP, ("seq", "head"), None),
        ),
        out_specs=(
            P(DP, ("seq", "head"), None),
            P(DP, ("seq", "head"), None),
            P(DP_SEQ_HEAD, None),
            P(None, DP_SEQ_HEAD),
            P(("seq", "head"), None, None),
            P(("seq", "head"), None),
            P(),
            P(),
            P(),
            P(),
        ),
        check_vma=False,
    )
```

time: 1350 us -> 443 us (0.33)
  waiting for transfers between devices: 954 us -> 6.67 us
  Pallas kernels: 0 us -> 275 us
  matrix products: 149 us -> 26.7 us
  blocking collectives: 65.8 us -> 0 us
  other arithmetic: 68.6 us -> 43 us
  starting transfers between devices: 22.1 us -> 0.12 us
    reduce_scatter x3 -> x1, waiting for transfers between devices: 793 us -> 0.01 us  [body(): lax.psum_scatter(outp.reshape(n_seq * n_head * count, width), ('seq', 'he...]
    pallas_call x0 -> x4, Pallas kernels: none -> 275 us  [the longest x1 107 us: ffn(): pl.pallas_call(ffn_kernel, out_shape=(jax.ShapeDtypeStruct((4, 4, 2, BLOC...]
    dot_general x40 -> x4, matrix products: 149 us -> 26.7 us  [the longest x1 9.43 us: body(): lax.dot_general(d_qkv, w_qkv, (((1,), (1,)), ((), ())), preferred_element...]
    all_gather x2 -> x1, waiting for transfers between devices: 127 us -> 5.29 us  [body(): dy_all = lax.all_gather(d_out[None], ('seq', 'head'), axis=0, tiled=True)]
    psum x4 -> x0, blocking collectives: 55.3 us -> none  [one_axis_at_a_time(): array = lax.psum(array, axis)]
    all_to_all x5 -> x0, waiting for transfers between devices: 28.7 us -> none  [the longest x1 12.2 us: body(): lax.all_to_all(by_slot, 'head', split_axis=2, concat_axis=1, tiled=True)]
    concatenate x3 -> x1, other arithmetic: 27.7 us -> 0.74 us  [body(): jnp.concatenate([k_rot, v_raw], -1).astype(bf16)]
    all_to_all x5 -> x0, starting transfers between devices: 21.9 us -> none  [the longest x1 4.66 us: sum_at_owner(): lax.all_to_all(in_blocks(array, dim, peers), axis, 0, 0, tiled=True)]
  transfers between devices with their start and end apart: 11 -> 3, of which waited for: 9 -> 1; matrix products, arithmetic and copies ran while one was open for 12% -> 30% of each run, Pallas kernels for 0% -> 38%
where the time goes in v1:
time: 443 us; the launch traced here: 438 us
  Pallas kernels  275 us (62%)
  local copies, waits for them, and re-layouts  72.1 us (16%)
  other arithmetic  43 us (10%)
  matrix products  26.7 us (6%)
  between operations  14.5 us (3%)
  waiting for transfers between devices  6.67 us (2%)
    pallas_call x1, Pallas kernels, ffn(): pl.pallas_call(ffn_kernel, out_shape=(jax.ShapeDtypeStruct((4, 4, 2, BLOC...  107 us
    pallas_call x1, Pallas kernels, projections(): pl.pallas_call(projections_kernel, out_shape=(jax.ShapeDtypeStruct((16, c...  69.1 us
    pallas_call x1, Pallas kernels, attend(): pl.pallas_call(attend_kernel, out_shape=(jax.ShapeDtypeStruct(q.shape, bf...  52.3 us
    pallas_call x1, Pallas kernels, attend_back(): pl.pallas_call(attend_back_kernel, out_shape=(jax.ShapeDtypeStruct(q.shap...  46.8 us
    mul x6, local copies, waits for them, and re-layouts, rms_parts(): return (v * inverse, inverse)  12.1 us
    mul x6, local copies, waits for them, and re-layouts, rms_back(): normed * jnp.mean(grad * normed, axis=-1, keepdims=True)  9.57 us
    concatenate x4, local copies, waits for them, and re-layouts, rotate(): jnp.concatenate([first * cosine - second * sine, second * cosine + first...  9.49 us
    dot_general x1, matrix products, body(): lax.dot_general(d_qkv, w_qkv, (((1,), (1,)), ((), ())), preferred_element...  9.43 us
  transfers between devices with their start and end apart: 3, of which 1 were waited for; matrix products, arithmetic and copies ran while one was open for 30% of the time, Pallas kernels for 38%

profile of v1, /device:TPU:0, one launch (start us, length us, event | category | flops | bytes accessed | tf_op | source)
XLA Modules:
  0.0 438.1 jit_solution(5352169199076149209)
XLA Ops:
  11.1 6.0 %fusion.5 = f32[128,2688]{1,0:T(8,128)S(1)} fusion(bf16[128,2048]{1,0:T(8,128)(2,1)S(1)} %multiply_convert_fusion.1.h1_ref, bf16[2048,2688]{1,0:T(8,128)(2,1)} %param.12), kind=kOutput, calls=%fused_computation.60 | convolution fusion | flops 1409286144 | bytes 12910592 | tf_op jit(solution)/shard_map/dot_general | solution.py:874
  29.0 5.6 %copy.94 = bf16[2,448,2048]{2,1,0:T(8,128)(2,1)} copy(bf16[2,448,2048]{2,0,1:T(2,128)(2,1)} %bitcast.87) | data formatting | bytes 7340032 | tf_op jit(solution)/shard_map/transpose | solution.py:869
  34.6 52.3 %attend.1 = (bf16[128,1792]{1,0:T(8,128)(2,1)}, bf16[8,4,64,896]{3,2,1,0:T(8,128)(2,1)}) custom-call(s32[2,4]{1,0:T(2,128)} %starts_ref.3, bf16[128,1792]{1,0:T(8,128)(2,1)} %copy.93.q_ref, bf16[2,64,896]{2,1,0:T(8,128)(2,1)} %copy.112.kv_ref), custom_call_target="tpu_custom_call" | custom-call | tf_op jit(solution)/shard_map/attend/pallas_call | solution.py:505
  87.0 4.6 %multiply_reduce_fusion.5 = (f32[128]{0:T(128)S(1)}, f32[128,2048]{1,0:T(8,128)S(1)}) fusion(bf16[128,1792]{1,0:T(8,128)(2,1)} %get-tuple-element.20.mix_ref, bf16[1792,2048]{1,0:T(8,128)(2,1)} %param.13, bf16[128,2048]{1,0:T(8,128)(2,1)S(1)} %bitcast.84), kind=kOutput, calls=%fused_computation.18 | convolution fusion | flops 940572544 | bytes 9372160 | tf_op jit(solution)/shard_map/dot_general | solution.py:884
  92.5 5.3 %all-gather.3.cloned.1.call-done = bf16[32,64,2048]{2,1,0:T(8,128)(2,1)} async-done(((bf16[2,64,2048]{2,1,0:T(8,128)(2,1)}), bf16[32,64,2048]{2,1,0:T(8,128)(2,1)}) %all-gather.3.cloned.1.call-update) | async-done | bytes 8388624 | tf_op jit(solution)/shard_map/all_gather | solution.py:867
  97.8 106.8 %ffn.1 = (bf16[4,4,2,64,2048]{4,3,2,1,0:T(8,128)(2,1)}, f32[2,64,2048]{2,1,0:T(8,128)}, bf16[896,2048]{1,0:T(8,128)(2,1)}, bf16[448,2048]{1,0:T(8,128)(2,1)}) custom-call(bf16[2,64,2048]{2,1,0:T(8,128)(2,1)} %bitcast.89, bf16[4,4,2,64,2048]{4,3,2,1,0:T(8,128)(2,1)} %bitcast.85, bf16[896,2048]{1,0:T(8,128)(2,1)} %bitcast.82, bf16[448,2048]{1,0:T(8,128)(2,1)} %wdn_ref.1), custom_call_target="tpu_custom_call" | custom-call | tf_op jit(solution)/shard_map/ffn/pallas_call | solution.py:388
  204.6 7.6 %copy.116 = bf16[2,448,2048]{2,0,1:T(2,128)(2,1)} copy(bf16[2,448,2048]{2,1,0:T(8,128)(2,1)} %bitcast.88) | data formatting | bytes 7340032 | tf_op jit(solution)/shard_map/reshape | solution.py:897
  213.9 2.0 mul.429
  219.5 3.3 mul.412
  222.8 2.4 copy.100
  225.9 2.3 fusion
  228.6 6.7 %convolution_convert_fusion.do_ref = bf16[128,1792]{1,0:T(8,128)(2,1)} fusion(bf16[128,2048]{1,0:T(8,128)(2,1)S(1)} %fusion.2.da_ref, bf16[1792,2048]{1,0:T(8,128)(2,1)} %param.13), kind=kOutput, calls=%fused_computation.2 | convolution fusion | flops 939753472 | bytes 8323072 | tf_op jit(solution)/shard_map/dot_general | solution.py:901
  235.3 46.8 %attend_back.1 = (bf16[128,1792]{1,0:T(8,128)(2,1)}, bf16[2,64,896]{2,1,0:T(8,128)(2,1)}) custom-call(s32[2,4]{1,0:T(2,128)} %starts_ref.3, bf16[128,1792]{1,0:T(8,128)(2,1)} %copy.93.q_ref, bf16[128,1792]{1,0:T(8,128)(2,1)} %convolution_convert_fusion.do_ref, bf16[8,4,64,896]{3,2,1,0:T(8,128)(2,1)} %get-tuple-element.23.kva_ref), custom_call_target="tpu_custom_call" | custom-call | tf_op jit(solution)/shard_map/attend_back/pallas_call | solution.py:574
  282.1 1.9 reshape.262
  284.1 1.9 fusion.3
  286.0 1.9 copy.114
  291.6 2.0 mul.443
  295.3 2.0 concatenate.29
  299.1 2.2 copy.96
  301.2 3.2 reshape.270
  304.5 2.4 multiply_subtract_fusion
  306.9 4.3 pad_maximum_fusion
  311.7 2.0 mul.426
  313.7 2.4 copy.99
  316.2 3.3 concatenate.27
  319.5 2.4 copy.97
  324.6 2.7 multiply_reduce_fusion.7
  330.1 9.4 %multiply_reduce_fusion.2 = (f32[2048]{0:T(1024)S(1)}, f32[128]{0:T(128)S(1)}, f32[128,2048]{1,0:T(8,128)}) fusion(bf16[2,64,2048]{2,1,0:T(8,128)(2,1)S(1)} %copy-done, f32[128]{0:T(128)} %copy-done.20, f32[2048]{0:T(1024)S(1)} %copy-done.14, bf16[128,2688]{1,0:T(8,128)(2,1)S(1)} %concatenate.30.dqkv_ref, bf16[2048,2688]{1,0:T(8,128)(2,1)} %param.12), kind=kOutput, calls=%fused_computation.12 | convolution fusion | flops 1411118976 | bytes 13288448 | tf_op jit(solution)/shard_map/dot_general | solution.py:923
  340.3 69.1 %projections.1 = (f32[16,4480]{1,0:T(8,128)}, f32[40,128]{1,0:T(8,128)}) custom-call(bf16[128,2048]{1,0:T(8,128)(2,1)} %copy-done.8, bf16[128,2048]{1,0:T(8,128)(2,1)} %copy-done.9, bf16[128,2688]{1,0:T(8,128)(2,1)} %copy-done.7, bf16[128,1792]{1,0:T(8,128)(2,1)} %get-tuple-element.20.mix_ref, f32[40,128]{1,0:T(8,128)} %pad_bitcast_fusion.gain_ref), custom_call_target="tpu_custom_call" | custom-call | tf_op jit(solution)/shard_map/projections/pallas_call | solution.py:800
  415.2 9.4 %transpose.32 = f32[448,2,2048]{2,1,0:T(2,128)} convert(bf16[448,2,2048]{2,1,0:T(2,128)(2,1)} %get-tuple-element.34) | non-fusion elementwise | flops 1835008 | bytes 11010048 | tf_op jit(solution)/shard_map/transpose | solution.py:897
  424.6 3.9 convert_element_type.96
  428.5 2.9 add_convert_fusion
  (120 shorter events, 42.5 us)
Async XLA Ops:
  7.2 90.6 %all-gather.3.cloned.1.call-start = ((), (), s32[]{:S(2)}) async-start(), calls=%async_computation.2 | async-start | bytes 8912896 | tf_op jit(solution)/shard_map/all_gather | solution.py:867
  7.9 407.3 %all-reduce.4.cloned.1.call-start = ((), (), s32[]{:S(2)}) async-start(), calls=%async_computation.3 | async-start | bytes 11010048 | tf_op jit(solution)/shard_map/psum | solution.py:894
  9.3 0.6 copy-start.20
  11.1 6.0 %copy-start.8 = (bf16[128,2048]{1,0:T(8,128)(2,1)}, bf16[128,2048]{1,0:T(8,128)(2,1)S(1)}, u32[]{:S(2)}) copy-start(bf16[128,2048]{1,0:T(8,128)(2,1)S(1)} %multiply_convert_fusion.1.h1_ref) | copy-start | bytes 1572868
  17.1 1.1 copy-start.1
  17.3 1.7 copy-start.18
  18.2 2.0 copy-start.5
  18.5 3.3 slice-start
  22.1 2.0 copy-start.19
  29.0 58.0 %copy-start = (bf16[2,64,2048]{2,1,0:T(8,128)(2,1)S(1)}, bf16[2,64,2048]{2,1,0:T(8,128)(2,1)}, u32[]{:S(2)}) copy-start(bf16[2,64,2048]{2,1,0:T(8,128)(2,1)} %param.11) | copy-start | bytes 1572868
  87.0 4.6 %copy-start.13 = (f32[2048]{0:T(1024)S(1)}, f32[2048]{0:T(1024)}, u32[]{:S(2)}) copy-start(f32[2048]{0:T(1024)} %param.17) | copy-start | bytes 24580
  91.5 136.7 %copy-start.16 = (f32[128]{0:T(128)}, f32[128]{0:T(128)S(1)}, u32[]{:S(2)}) copy-start(f32[128]{0:T(128)S(1)} %add_rsqrt_fusion.3) | copy-start | bytes 1540
  212.3 216.2 %reduce-scatter.2.cloned.1.call-start = ((), (), s32[]{:S(2)}) async-start(), calls=%async_computation.1 | async-start | bytes 8912896 | tf_op jit(solution)/shard_map/reduce_scatter | solution.py:890
  225.9 2.3 copy-start.3
  225.9 2.3 copy-start.10
  228.2 7.1 %copy-start.22 = (f32[128]{0:T(128)}, f32[128]{0:T(128)S(1)}, u32[]{:S(2)}) copy-start(f32[128]{0:T(128)S(1)} %broadcast_multiply_fusion.3) | copy-start | bytes 1540
  228.6 6.7 %copy-start.9 = (bf16[128,2048]{1,0:T(8,128)(2,1)}, bf16[128,2048]{1,0:T(8,128)(2,1)S(1)}, u32[]{:S(2)}) copy-start(bf16[128,2048]{1,0:T(8,128)(2,1)S(1)} %fusion.2.da_ref) | copy-start | bytes 1572868
  287.9 1.4 copy-start.6
  316.1 5.7 %copy-start.12 = (bf16[2,64,7,64]{3,2,1,0:T(8,128)(2,1)S(1)}, bf16[2,64,7,64]{3,2,1,0:T(8,128)(2,1)}, u32[]{:S(2)}) copy-start(bf16[2,64,7,64]{3,2,1,0:T(8,128)(2,1)} %get-tuple-element.54) | copy-start | bytes 344068
  316.1 5.9 %copy-start.2 = (f32[128,2688]{1,0:T(8,128)S(1)}, f32[128,2688]{1,0:T(8,128)}, u32[]{:S(2)}) copy-start(f32[128,2688]{1,0:T(8,128)} %copy-done.1) | copy-start | bytes 4128772
  324.6 5.5 %copy-start.14 = (f32[2048]{0:T(1024)S(1)}, f32[2048]{0:T(1024)}, u32[]{:S(2)}) copy-start(f32[2048]{0:T(1024)} %param.16) | copy-start | bytes 24580
  330.1 9.5 %copy-start.7 = (bf16[128,2688]{1,0:T(8,128)(2,1)}, bf16[128,2688]{1,0:T(8,128)(2,1)S(1)}, u32[]{:S(2)}) copy-start(bf16[128,2688]{1,0:T(8,128)(2,1)S(1)} %concatenate.30.dqkv_ref) | copy-start | bytes 2064388
  330.1 9.4 %copy-start.15 = (f32[2048]{0:T(1024)S(1)}, f32[2048]{0:T(1024)}, u32[]{:S(2)}) copy-start(f32[2048]{0:T(1024)} %get-tuple-element.30) | copy-start | bytes 24580
  424.6 3.9 copy-start.4
  424.6 3.9 copy-start.11
  424.6 3.9 copy-start.17
  424.6 3.9 copy-start.21
  424.6 3.9 copy-start.23
Sparse Core Ops, SparseCore 0:
  10.2 87.6 all-gather.2
  212.4 78.1 all-reduce.3
  294.1 92.4 reduce-scatter.1

commit v2 on v1

--- a/solution.py
+++ b/solution.py
@@ -22,7 +22,7 @@
 SCALE = 0.125
 f32 = jnp.float32
 bf16 = jnp.bfloat16
-VMEM_BYTES = 60 * 2**20
+VMEM_BYTES = 62 * 2**20
 
 
 def nt(a, b):
@@ -41,7 +41,7 @@
     return lax.rem(index + (by + RING), RING)
 
 
-def barrier_with(axes):
+def barrier_with(axes, core=False):
     barrier = pltpu.get_barrier_semaphore()
     for axis in axes:
         index = lax.axis_index(axis)
@@ -49,7 +49,10 @@
             pl.semaphore_signal(
                 barrier, inc=1, device_id={axis: shift(index, by)}, device_id_type=MESH
             )
-    pl.semaphore_wait(barrier, 2 * len(axes))
+    if core:
+        other = 1 - lax.axis_index("dp_1")
+        pl.semaphore_signal(barrier, inc=1, device_id={"dp_1": other}, device_id_type=MESH)
+    pl.semaphore_wait(barrier, 2 * len(axes) + int(core))
 
 
 class Copies:
@@ -71,6 +74,19 @@
         self.started.append(copy)
         return copy
 
+    def start_to_core(self, slot, src, dst):
+        copy = pltpu.make_async_remote_copy(
+            src_ref=src,
+            dst_ref=dst,
+            send_sem=self.send.at[slot],
+            recv_sem=self.recv.at[slot],
+            device_id={"dp_1": 1 - lax.axis_index("dp_1")},
+            device_id_type=MESH,
+        )
+        copy.start()
+        self.started.append(copy)
+        return copy
+
     def finish(self):
         for copy in self.started:
             copy.wait_send()
@@ -205,6 +221,72 @@
     ]
 
 
+class RingSum:
+    def __init__(self, copies, base, axis, part, half_land, full_land):
+        self.c = copies
+        self.base = base
+        self.axis = axis
+        self.part = part
+        self.hl = half_land
+        self.fl = full_land
+        self.i = lax.axis_index(axis)
+
+    def step1(self):
+        far = self.part.at[shift(self.i, 2)]
+        n = far.shape[0] // 2
+        self.a = self.c.start(self.base, far.at[pl.ds(0, n)], self.hl.at[0], self.axis, 1)
+        self.b = self.c.start(self.base + 1, far.at[pl.ds(n, n)], self.hl.at[1], self.axis, -1)
+
+    def step2(self):
+        for copy, by, side in ((self.a, 1, 0), (self.b, -1, 1)):
+            copy.wait_recv()
+            block = self.part.at[shift(self.i, by)]
+            n = block.shape[0] // 2
+            half = block.at[pl.ds(n * side, n)]
+            half[...] = (half[...].astype(f32) + self.hl[side].astype(f32)).astype(bf16)
+            new = self.c.start(self.base + 2 + side, block, self.fl.at[side], self.axis, by)
+            if side == 0:
+                self.a = new
+            else:
+                self.b = new
+
+    def finish(self):
+        self.a.wait_recv()
+        self.b.wait_recv()
+        own = self.part.at[self.i]
+        own[...] = (
+            own[...].astype(f32) + self.fl[0].astype(f32) + self.fl[1].astype(f32)
+        ).astype(bf16)
+        return own
+
+
+class RingGather:
+    def __init__(self, copies, base, axis, full):
+        self.c = copies
+        self.base = base
+        self.axis = axis
+        self.full = full
+        self.i = lax.axis_index(axis)
+
+    def step1(self):
+        own = self.full.at[self.i]
+        self.a = self.c.start(self.base, own, own, self.axis, 1)
+        self.b = self.c.start(self.base + 1, own, own, self.axis, -1)
+
+    def step2(self):
+        n = self.full.shape[1] // 2
+        self.a.wait_recv()
+        left = self.full.at[shift(self.i, -1), pl.ds(0, n)]
+        self.a = self.c.start(self.base + 2, left, left, self.axis, 1)
+        self.b.wait_recv()
+        right = self.full.at[shift(self.i, 1), pl.ds(n, n)]
+        self.b = self.c.start(self.base + 3, right, right, self.axis, -1)
+
+    def finish(self):
+        self.a.wait_recv()
+        self.b.wait_recv()
+
+
 def ffn_kernel(
     h2_ref,
     dy_ref,
@@ -212,10 +294,10 @@
     wdn_ref,
     outp_ref,
     dh2_ref,
-    gin_ref,
-    gdn_ref,
+    gsum_ref,
     h2a,
     dya,
+    pairs,
     win,
     wdn,
     hid,
@@ -226,38 +308,45 @@
     l3,
     l4,
     stage,
-    gstage,
+    gst,
+    gland,
     send,
     recv,
     lsem,
     osem,
-    gsem,
 ):
     units = wdn.shape[0]
     width = wdn.shape[1]
     copies = Copies(send, recv)
     weights = [
-        pltpu.make_async_copy(win_ref, win, lsem.at[8]),
-        pltpu.make_async_copy(wdn_ref, wdn, lsem.at[9]),
+        pltpu.make_async_copy(win_ref.at[pl.ds(0, units // 2)], pairs, lsem.at[0]),
+        pltpu.make_async_copy(win_ref.at[pl.ds(units // 2, units // 2)], pairs, lsem.at[4]),
+        pltpu.make_async_copy(wdn_ref, wdn, lsem.at[1]),
     ]
-    for copy in weights:
-        copy.start()
-    loads = []
-    for j in range(4):
-        loads.append(pltpu.make_async_copy(dy_ref.at[j, :, 0], dya.at[j], lsem.at[j]))
-        loads.append(pltpu.make_async_copy(dy_ref.at[:, j, 1], dya.at[4 + j], lsem.at[4 + j]))
-    for copy in loads:
-        copy.start()
-    barrier_with(("seq", "head"))
+    weights[0].start()
+    weights[2].start()
+    load = pltpu.make_async_copy(dy_ref, dya, lsem.at[2])
+    load.start()
+    barrier_with(("seq", "head"), core=True)
     gathers = [PlaneGather(copies, 0, half, h2_ref.at[half], h2a) for half in (0, 1)]
     for gather in gathers:
         gather.step1()
     for half in (0, 1):
         h2a[gathers[half].row(), gathers[half].i] = h2_ref[half]
+
+    def split_pairs(first):
+        win[first : first + units // 2] = pairs[:, 0, :]
+        win[units + first : units + first + units // 2] = pairs[:, 1, :]
+
+    weights[0].wait()
+    split_pairs(0)
+    weights[1].start()
     for gather in gathers:
         gather.step2()
-    for copy in weights + loads:
-        copy.wait()
+    weights[1].wait()
+    split_pairs(units // 2)
+    weights[2].wait()
+    load.wait()
     for gather in gathers:
         gather.step3()
     seq, head = lax.axis_index("seq"), lax.axis_index("head")
@@ -321,38 +410,22 @@
     def _(half):
         back(group(half, 0))
 
-    tile = gstage.shape[2]
-    tiles = width // tile
+    tile = gland.shape[2]
+    half_rows = gland.shape[1]
     tokens = 8 * 4 * BLOCK
-    gcopies = []
-    for n in range(tiles):
+    core = lax.axis_index("dp_1")
+    mine = pl.ds(pl.multiple_of(core * half_rows, 16), half_rows)
+    theirs = pl.ds(pl.multiple_of((1 - core) * half_rows, 16), half_rows)
+    swaps = []
+    for n in range(gland.shape[0]):
         cols = pl.ds(n * tile, tile)
-        if n >= 2:
-            for copy in gcopies[n - 2]:
-                copy.wait()
-        slot = n % 2
-        gstage[slot, : 2 * units] = nn(
-            dbo[...], h2a[:, :, :, cols].reshape(tokens, tile)
-        ).astype(bf16)
-        gstage[slot, 2 * units :] = nn(
-            hid[...], dya[:, :, :, cols].reshape(tokens, tile)
-        ).astype(bf16)
-        pair = [
-            pltpu.make_async_copy(
-                gstage.at[slot, pl.ds(0, 2 * units)], gin_ref.at[:, cols], gsem.at[slot, 0]
-            ),
-            pltpu.make_async_copy(
-                gstage.at[slot, pl.ds(2 * units, units)], gdn_ref.at[:, cols], gsem.at[slot, 1]
-            ),
-        ]
-        for copy in pair:
-            copy.start()
-        gcopies.append(pair)
+        gst[n, : 2 * units] = nn(dbo[...], h2a[:, :, :, cols].reshape(tokens, tile)).astype(bf16)
+        gst[n, 2 * units :] = nn(hid[...], dya[:, :, :, cols].reshape(tokens, tile)).astype(bf16)
+        swaps.append(
+            copies.start_to_core(32 + n, gst.at[n, theirs], gland.at[n])
+        )
     for total in sums:
         total.step3()
-    for pair in gcopies[-2:]:
-        for copy in pair:
-            copy.wait()
 
     def out_copy(q):
         slot = q % 2
@@ -374,8 +447,14 @@
         out_part(q)
     for half in (0, 1):
         dh2_ref[half] = sums[half].result()
+    for n, swap in enumerate(swaps):
+        swap.wait_recv()
+        gland[n] = (gst[n, mine].astype(f32) + gland[n].astype(f32)).astype(bf16)
+    keep = pltpu.make_async_copy(gland, gsum_ref, lsem.at[3])
+    keep.start()
     out_copy(6).wait()
     out_copy(7).wait()
+    keep.wait()
     copies.finish()
 
 
@@ -390,14 +469,14 @@
         out_shape=(
             jax.ShapeDtypeStruct((4, 4, 2, BLOCK, width), bf16),
             jax.ShapeDtypeStruct((2, BLOCK, width), f32),
-            jax.ShapeDtypeStruct((2 * units, width), bf16),
-            jax.ShapeDtypeStruct((units, width), bf16),
+            jax.ShapeDtypeStruct((width // tile, 3 * units // 2, tile), bf16),
         ),
         in_specs=[vmem_spec, any_spec, any_spec, any_spec],
-        out_specs=(any_spec, vmem_spec, any_spec, any_spec),
+        out_specs=(any_spec, vmem_spec, any_spec),
         scratch_shapes=[
             pltpu.VMEM((8, 4, BLOCK, width), bf16),
             pltpu.VMEM((8, 4, BLOCK, width), bf16),
+            pltpu.VMEM((units // 2, 2, width), bf16),
             pltpu.VMEM((2 * units, width), bf16),
             pltpu.VMEM((units, width), bf16),
             pltpu.VMEM((units, tokens), bf16),
@@ -405,12 +484,12 @@
             pltpu.VMEM((8, 4, BLOCK, width), bf16),
             *sum_landings(width),
             pltpu.VMEM((2, 4, BLOCK, width), bf16),
-            pltpu.VMEM((2, 3 * units, tile), bf16),
-            pltpu.SemaphoreType.DMA((32,)),
-            pltpu.SemaphoreType.DMA((32,)),
-            pltpu.SemaphoreType.DMA((10,)),
+            pltpu.VMEM((width // tile, 3 * units, tile), bf16),
+            pltpu.VMEM((width // tile, 3 * units // 2, tile), bf16),
+            pltpu.SemaphoreType.DMA((36,)),
+            pltpu.SemaphoreType.DMA((36,)),
+            pltpu.SemaphoreType.DMA((5,)),
             pltpu.SemaphoreType.DMA((2,)),
-            pltpu.SemaphoreType.DMA((2, 2)),
         ],
         compiler_params=pltpu.CompilerParams(
             collective_id=1, has_side_effects=True, vmem_limit_bytes=VMEM_BYTES
@@ -461,193 +540,553 @@
     return e.reshape(PER_GROUP * BLOCK, keys)
 
 
-def attend_kernel(starts_ref, q_ref, kv_ref, o_ref, kva_ref, kva, mask, send, recv, lsem):
+GROUP_COLS = PER_GROUP * HD
+KV_COLS = 2 * HD
+
+
+def head_means(columns=GROUP_COLS):
+    a = lax.div(lax.broadcasted_iota(jnp.int32, (columns, columns), 0), HD)
+    b = lax.div(lax.broadcasted_iota(jnp.int32, (columns, columns), 1), HD)
+    return jnp.where(a == b, 1.0 / HD, 0.0).astype(f32)
+
+
+def head_mean(v, means):
+    return jnp.dot(v, means, precision=lax.Precision.HIGHEST, preferred_element_type=f32)
+
+
+def swapped(v):
+    columns = v.shape[1]
+    lane = lax.rem(lax.broadcasted_iota(jnp.int32, v.shape, 1), HD)
+    up = pltpu.roll(v, columns - HD // 2, 1)
+    down = pltpu.roll(v, HD // 2, 1)
+    return jnp.where(lane < HD // 2, up, down)
+
+
+def turned(raw, gain, cosine, sine, means):
+    normed = raw * lax.rsqrt(head_mean(raw * raw, means) + EPS)
+    v = normed * gain
+    return v * cosine + swapped(v) * sine
+
+
+def turned_back(grad, raw, gain, cosine, sine, means):
+    inverse = lax.rsqrt(head_mean(raw * raw, means) + EPS)
+    normed = raw * inverse
+    u = grad * cosine - swapped(grad) * sine
+    gain_grad = jnp.sum(u * normed, axis=0, keepdims=True)
+    e = u * gain
+    return inverse * (e - normed * head_mean(e * normed, means)), gain_grad
+
+
+def rms_parts(v):
+    inverse = lax.rsqrt(jnp.mean(v * v, axis=-1, keepdims=True) + EPS)
+    return (v * inverse, inverse)
+
+
+def rms_back(grad, normed, inverse):
+    return inverse * (grad - normed * jnp.mean(grad * normed, axis=-1, keepdims=True))
+
+
+def front_kernel(
+    starts_ref,
+    x_ref,
+    wqkv_ref,
+    wout_ref,
+    ga_ref,
+    gf_ref,
+    qg_ref,
+    kg_ref,
+    cos_ref,
+    sin_ref,
+    dy_ref,
+    h1_ref,
+    raw_ref,
+    q_ref,
+    kva_ref,
+    mixed_ref,
+    r1_ref,
+    h2_ref,
+    dya_ref,
+    wq,
+    wkv,
+    wo,
+    own,
+    kva,
+    dya,
+    qst,
+    mask,
+    oacc,
+    lacc,
+    send,
+    recv,
+    lsem,
+):
+    count, width = x_ref.shape
+    q_cols = HEADS * HD
+    k_cols = KV * HD
+    loads = [
+        pltpu.make_async_copy(wqkv_ref.at[:, pl.ds(q_cols, 2 * k_cols)], wkv, lsem.at[0]),
+        pltpu.make_async_copy(wqkv_ref.at[:, pl.ds(0, q_cols)], wq, lsem.at[1]),
+        pltpu.make_async_copy(wout_ref, wo, lsem.at[2]),
+    ]
+    for load in loads:
+        load.start()
     copies = Copies(send, recv)
     barrier_with(("seq", "head"))
-    gathers = [PlaneGather(copies, 0, half, kv_ref.at[half], kva) for half in (0, 1)]
+    cotangents = [PlaneGather(copies, 16, half, dy_ref.at[half], dya) for half in (0, 1)]
+    for gather in cotangents:
+        gather.step1()
+    for half in (0, 1):
+        dya[cotangents[half].row(), cotangents[half].i] = dy_ref[half]
+    means = head_means()
+    cosine, sine = cos_ref[...], sin_ref[...]
+    x = x_ref[...].astype(f32)
+    h1_ref[...] = (rms_parts(x)[0] * ga_ref[...]).astype(bf16)
+    loads[0].wait()
+    kv = nn(h1_ref[...], wkv[...])
+    raw_ref[:, q_cols:] = kv
+    keys = jnp.concatenate(
+        [
+            turned(kv[:, c : c + GROUP_COLS], kg_ref[...], cosine, sine, means)
+            for c in (0, GROUP_COLS)
+        ],
+        1,
+    )
+    for g in range(KV):
+        k = keys[:, g * HD : (g + 1) * HD]
+        v = kv[:, k_cols + g * HD : k_cols + (g + 1) * HD]
+        own[:, :, g * KV_COLS : (g + 1) * KV_COLS] = (
+            jnp.concatenate([k, v], 1).astype(bf16).reshape(2, BLOCK, KV_COLS)
+        )
+    gathers = [PlaneGather(copies, 0, half, own.at[half], kva) for half in (0, 1)]
     for gather in gathers:
         gather.step1()
     for half in (0, 1):
-        kva[gathers[half].row(), gathers[half].i] = kv_ref[half]
+        kva[gathers[half].row(), gathers[half].i] = own[half]
+    for gather in cotangents:
+        gather.step2()
+    loads[1].wait()
+
+    def queries(g):
+        cols = slice(g * GROUP_COLS, (g + 1) * GROUP_COLS)
+        raw = nn(h1_ref[...], wq[:, cols])
+        raw_ref[:, cols] = raw
+        q = turned(raw, qg_ref[...], cosine, sine, means).astype(bf16)
+        q_ref[:, cols] = q
+        for row in (0, 1):
+            qst[row * KV + g] = stacked(q[row * BLOCK : (row + 1) * BLOCK], 0)
+
+    for g in range(3):
+        queries(g)
+    for gather in gathers:
+        gather.step2()
+    for g in range(3, KV):
+        queries(g)
+    for gather in gathers:
+        gather.step3()
     mask_rows(starts_ref, 0, False, mask)
     mask_rows(starts_ref, 1, True, mask)
-    for gather in gathers:
-        gather.step2()
-    for gather in gathers:
-        gather.step3()
+    seq, head = lax.axis_index("seq"), lax.axis_index("head")
+
+    def scored(row, by, first):
+        group = lax.rem(seq + row * (head - seq) + by + 4, 4)
+        seen = mask[row, :, pl.ds(pl.multiple_of(group * 4 * BLOCK, 4 * BLOCK), 4 * BLOCK)]
+        for g in range(KV):
+            index = row * KV + g
+            kv_rows = kva[
+                4 * row + group, :, :, g * KV_COLS : (g + 1) * KV_COLS
+            ].reshape(4 * BLOCK, KV_COLS)
+            e = weights_of(qst[index], kv_rows, seen)
+            total = e[:, : 2 * BLOCK] + e[:, 2 * BLOCK :]
+            mixed = nn(e.astype(bf16), kv_rows)
+            if first:
+                lacc[index] = total
+                oacc[index] = mixed
+            else:
+                lacc[index] += total
+                oacc[index] += mixed
+
+    @pl.loop(0, 2)
+    def _(row):
+        scored(row, 0, True)
+
     for gather in gathers:
         gather.step4()
+    for gather in cotangents:
+        gather.step3()
+
+    @pl.loop(0, 4)
+    def _(k):
+        scored(lax.div(k, 2), 1 - 2 * lax.rem(k, 2), False)
+
     for gather in gathers:
         gather.finish()
-    keep = pltpu.make_async_copy(kva, kva_ref, lsem)
+    keep = pltpu.make_async_copy(kva, kva_ref, lsem.at[3])
     keep.start()
 
     @pl.loop(0, 2)
     def _(row):
+        scored(row, 2, False)
+
+    for row in (0, 1):
         for g in range(KV):
-            rows = pl.ds(pl.multiple_of(row * BLOCK, BLOCK), BLOCK)
-            cols = slice(g * PER_GROUP * HD, (g + 1) * PER_GROUP * HD)
-            q_rows = stacked(q_ref[rows, cols], 0)
-            kv_rows = kva[pl.ds(row * 4, 4), :, :, g * 2 * HD : (g + 1) * 2 * HD].reshape(
-                16 * BLOCK, 2 * HD
-            )
-            e = weights_of(q_rows, kv_rows, mask[row])
-            total = jnp.sum(e, axis=1, keepdims=True)
-            mixed = nn(e.astype(bf16), kv_rows)[:, HD:] / total
-            o_ref[rows, cols] = unstacked(mixed.astype(bf16))
-
+            index = row * KV + g
+            mixed = oacc[index][:, HD:] / jnp.sum(lacc[index], axis=1, keepdims=True)
+            mixed_ref[
+                row * BLOCK : (row + 1) * BLOCK, g * GROUP_COLS : (g + 1) * GROUP_COLS
+            ] = unstacked(mixed.astype(bf16))
+    loads[2].wait()
+    tile = 512
+    for n in range(width // tile):
+        cols = slice(n * tile, (n + 1) * tile)
+        r1_ref[:, cols] = x_ref[:, cols].astype(f32) + nn(mixed_ref[...], wo[:, cols])
+    for gather in cotangents:
+        gather.step4()
+    h2_ref[...] = (rms_parts(r1_ref[...])[0] * gf_ref[...]).astype(bf16)
+    keep.wait()
+    for gather in cotangents:
+        gather.finish()
+    keep = pltpu.make_async_copy(dya, dya_ref, lsem.at[4])
+    keep.start()
     keep.wait()
     copies.finish()
 
 
-def attend(starts, q, kv):
+def front(starts, x, w_qkv, w_out, g_attn, g_ffn, q_gain, k_gain, cosine, sine, dy):
+    count, width = x.shape
+    q_cols = HEADS * HD
+    kv_cols = 2 * KV * HD
     vmem_spec = pl.BlockSpec(memory_space=pltpu.VMEM)
+    any_spec = pl.BlockSpec(memory_space=pl.ANY)
     return pl.pallas_call(
-        attend_kernel,
+        front_kernel,
         out_shape=(
-            jax.ShapeDtypeStruct(q.shape, bf16),
-            jax.ShapeDtypeStruct((8, 4, BLOCK, kv.shape[2]), bf16),
+            jax.ShapeDtypeStruct((count, width), bf16),
+            jax.ShapeDtypeStruct((count, q_cols + kv_cols), f32),
+            jax.ShapeDtypeStruct((count, q_cols), bf16),
+            jax.ShapeDtypeStruct((8, 4, BLOCK, kv_cols), bf16),
+            jax.ShapeDtypeStruct((count, q_cols), bf16),
+            jax.ShapeDtypeStruct((count, width), f32),
+            jax.ShapeDtypeStruct((count, width), bf16),
+            jax.ShapeDtypeStruct((8, 4, BLOCK, width), bf16),
         ),
-        in_specs=[pl.BlockSpec(memory_space=pltpu.SMEM), vmem_spec, vmem_spec],
-        out_specs=(vmem_spec, pl.BlockSpec(memory_space=pl.ANY)),
+        in_specs=[
+            pl.BlockSpec(memory_space=pltpu.SMEM),
+            vmem_spec,
+            any_spec,
+            any_spec,
+            *[vmem_spec] * 7,
+        ],
+        out_specs=(
+            vmem_spec,
+            vmem_spec,
+            vmem_spec,
+            any_spec,
+            vmem_spec,
+            vmem_spec,
+            vmem_spec,
+            any_spec,
+        ),
         scratch_shapes=[
-            pltpu.VMEM((8, 4, BLOCK, kv.shape[2]), bf16),
+            pltpu.VMEM((width, q_cols), bf16),
+            pltpu.VMEM((width, kv_cols), bf16),
+            pltpu.VMEM((q_cols, width), bf16),
+            pltpu.VMEM((2, BLOCK, kv_cols), bf16),
+            pltpu.VMEM((8, 4, BLOCK, kv_cols), bf16),
+            pltpu.VMEM((8, 4, BLOCK, width), bf16),
+            pltpu.VMEM((2 * KV, PER_GROUP * BLOCK, KV_COLS), bf16),
             pltpu.VMEM((2, BLOCK, 16 * BLOCK), f32),
-            pltpu.SemaphoreType.DMA((16,)),
-            pltpu.SemaphoreType.DMA((16,)),
-            pltpu.SemaphoreType.DMA,
+            pltpu.VMEM((2 * KV, PER_GROUP * BLOCK, KV_COLS), f32),
+            pltpu.VMEM((2 * KV, PER_GROUP * BLOCK, 2 * BLOCK), f32),
+            pltpu.SemaphoreType.DMA((32,)),
+            pltpu.SemaphoreType.DMA((32,)),
+            pltpu.SemaphoreType.DMA((5,)),
         ],
         compiler_params=pltpu.CompilerParams(
             collective_id=2, has_side_effects=True, vmem_limit_bytes=VMEM_BYTES
         ),
-        name="attend",
-    )(starts, q, kv)
-
-
-def attend_back_kernel(
-    starts_ref, q_ref, do_ref, kva_ref, dq_ref, dkv_ref, kva, part, mask, l1, l2, l3, l4, send, recv, lsem
+        name="front",
+    )(starts, x, w_qkv, w_out, g_attn, g_ffn, q_gain, k_gain, cosine, sine, dy)
+
+
+def rear_kernel(
+    starts_ref,
+    dh2_ref,
+    r1_ref,
+    dy_ref,
+    x_ref,
+    q_ref,
+    raw_ref,
+    kva_ref,
+    wqkv_ref,
+    wout_ref,
+    gsum_ref,
+    ga_ref,
+    gf_ref,
+    qg_ref,
+    kg_ref,
+    cos_ref,
+    sin_ref,
+    da_ref,
+    dqkv_ref,
+    gx_ref,
+    gga_ref,
+    ggf_ref,
+    gq_ref,
+    gk_ref,
+    gall_ref,
+    wqkv,
+    wo,
+    kva,
+    gsum,
+    gfull,
+    gl1,
+    gl2,
+    part,
+    mask,
+    d_r1,
+    d_o,
+    dq,
+    d_h1,
+    l1,
+    l2,
+    l3,
+    l4,
+    send,
+    recv,
+    lsem,
 ):
+    count, width = x_ref.shape
+    q_cols = HEADS * HD
+    k_cols = KV * HD
+    loads = [
+        pltpu.make_async_copy(wout_ref, wo, lsem.at[0]),
+        pltpu.make_async_copy(kva_ref, kva, lsem.at[1]),
+        pltpu.make_async_copy(wqkv_ref, wqkv, lsem.at[2]),
+        pltpu.make_async_copy(gsum_ref, gsum, lsem.at[3]),
+    ]
+    for load in loads:
+        load.start()
     copies = Copies(send, recv)
-    load = pltpu.make_async_copy(kva_ref, kva, lsem)
-    load.start()
-    barrier_with(("seq", "head"))
+    barrier_with(("dp_0", "seq", "head"))
+    gring = RingSum(copies, 16, "dp_0", gsum, gl1, gl2)
+    gback = RingGather(copies, 20, "dp_0", gfull)
+    loads[3].wait()
+    gring.step1()
+    n2, inv2 = rms_parts(r1_ref[...])
+    d_h2 = dh2_ref[...]
+    ggf_ref[...] = jnp.sum(d_h2 * n2, axis=0, keepdims=True)
+    d_r1[...] = dy_ref[...].astype(f32) + rms_back(d_h2 * gf_ref[...], n2, inv2)
+    da_ref[...] = d_r1[...].astype(bf16)
     mask_rows(starts_ref, 0, False, mask)
     mask_rows(starts_ref, 1, True, mask)
-    load.wait()
+    loads[0].wait()
+    for g in range(KV):
+        cols = slice(g * GROUP_COLS, (g + 1) * GROUP_COLS)
+        d_o[:, cols] = nt(da_ref[...], wo[cols]).astype(bf16)
+    loads[1].wait()
+    gring.step2()
     sums = [PlaneSum(copies, 0, half, part, l1, l2, l3, l4) for half in (0, 1)]
-
-    @pl.loop(0, 2)
-    def _(row):
+    for row in (0, 1):
+        rows = slice(row * BLOCK, (row + 1) * BLOCK)
         for g in range(KV):
-            rows = pl.ds(pl.multiple_of(row * BLOCK, BLOCK), BLOCK)
-            cols = slice(g * PER_GROUP * HD, (g + 1) * PER_GROUP * HD)
-            lanes = slice(g * 2 * HD, (g + 1) * 2 * HD)
+            cols = slice(g * GROUP_COLS, (g + 1) * GROUP_COLS)
+            lanes = slice(g * KV_COLS, (g + 1) * KV_COLS)
             q_rows = stacked(q_ref[rows, cols], 0)
-            do_rows = stacked(do_ref[rows, cols], 1)
-            kv_rows = kva[pl.ds(row * 4, 4), :, :, lanes].reshape(16 * BLOCK, 2 * HD)
+            do_rows = stacked(d_o[rows, cols], 1)
+            kv_rows = kva[4 * row : 4 * row + 4, :, :, lanes].reshape(16 * BLOCK, KV_COLS)
             e = weights_of(q_rows, kv_rows, mask[row])
             probs = e * (1.0 / jnp.sum(e, axis=1, keepdims=True))
             d_probs = nt(do_rows, kv_rows)
             delta = jnp.sum(probs * d_probs, axis=1, keepdims=True)
             d_scores = (probs * (d_probs - delta)).astype(bf16)
-            dq = nn(d_scores, kv_rows)[:, :HD] * SCALE
-            dq_ref[rows, cols] = unstacked(dq.astype(bf16))
+            dq_rows = nn(d_scores, kv_rows)[:, :HD] * SCALE
+            dq[rows, cols] = unstacked(dq_rows.astype(bf16))
             dkv = tn(d_scores, q_rows * jnp.asarray(SCALE, bf16)) + tn(probs.astype(bf16), do_rows)
-            part[pl.ds(row * 4, 4), :, :, lanes] = dkv.astype(bf16).reshape(4, 4, BLOCK, 2 * HD)
-
-    for total in sums:
-        total.step1()
+            part[4 * row : 4 * row + 4, :, :, lanes] = dkv.astype(bf16).reshape(
+                4, 4, BLOCK, KV_COLS
+            )
+        sums[row].step1()
+        if row == 0:
+            gfull[gring.i] = gring.finish()[...]
+            gback.step1()
+    means = head_means()
+    cosine, sine = cos_ref[...], sin_ref[...]
+
+    def queries(g):
+        cols = slice(g * GROUP_COLS, (g + 1) * GROUP_COLS)
+        value, gain = turned_back(
+            dq[:, cols].astype(f32), raw_ref[:, cols], qg_ref[...], cosine, sine, means
+        )
+        dqkv_ref[:, cols] = value.astype(bf16)
+        return gain
+
+    gain = queries(0)
+    for g in range(1, KV):
+        gain += queries(g)
+    gq_ref[...] = gain
     for total in sums:
         total.step2()
+    gback.step2()
+    loads[2].wait()
+    tile = 512
+    for n in range(width // tile):
+        cols = slice(n * tile, (n + 1) * tile)
+        d_h1[:, cols] = nt(dqkv_ref[:, :q_cols], wqkv[cols, :q_cols])
     for total in sums:
         total.step3()
     for total in sums:
         total.step4()
-    for half in (0, 1):
-        dkv_ref[half] = sums[half].result().astype(bf16)
+    gback.finish()
+    keep = pltpu.make_async_copy(gfull, gall_ref, lsem.at[4])
+    keep.start()
+    d_kv = jnp.concatenate([total.result().astype(bf16) for total in sums], 0)
+    pieces = [d_kv[:, g * KV_COLS : g * KV_COLS + HD] for g in range(KV)]
+    pieces += [d_kv[:, g * KV_COLS + HD : (g + 1) * KV_COLS] for g in range(KV)]
+    d_kv = jnp.concatenate(pieces, 1)
+    first, gain1 = turned_back(
+        d_kv[:, :GROUP_COLS].astype(f32),
+        raw_ref[:, q_cols : q_cols + GROUP_COLS],
+        kg_ref[...],
+        cosine,
+        sine,
+        means,
+    )
+    second, gain2 = turned_back(
+        d_kv[:, GROUP_COLS : 2 * GROUP_COLS].astype(f32),
+        raw_ref[:, q_cols + GROUP_COLS : q_cols + 2 * GROUP_COLS],
+        kg_ref[...],
+        cosine,
+        sine,
+        means,
+    )
+    lane = lax.broadcasted_iota(jnp.int32, gain2.shape, 1)
+    gk_ref[...] = gain1 + jnp.where(lane < k_cols - GROUP_COLS, gain2, 0.0)
+    dqkv_ref[:, q_cols : q_cols + GROUP_COLS] = first.astype(bf16)
+    lane = lax.broadcasted_iota(jnp.int32, second.shape, 1)
+    dqkv_ref[:, q_cols + GROUP_COLS : q_cols + 2 * GROUP_COLS] = jnp.where(
+        lane < k_cols - GROUP_COLS,
+        second.astype(bf16),
+        d_kv[:, GROUP_COLS : 2 * GROUP_COLS],
+    )
+    dqkv_ref[:, q_cols + 2 * GROUP_COLS :] = d_kv[:, 2 * GROUP_COLS :]
+    for n in range(width // tile):
+        cols = slice(n * tile, (n + 1) * tile)
+        d_h1[:, cols] += nt(dqkv_ref[:, q_cols:], wqkv[cols, q_cols:])
+    n1, inv1 = rms_parts(x_ref[...].astype(f32))
+    gga_ref[...] = jnp.sum(d_h1[...] * n1, axis=0, keepdims=True)
+    gx_ref[...] = (d_r1[...] + rms_back(d_h1[...] * ga_ref[...], n1, inv1)).astype(bf16)
+    keep.wait()
     copies.finish()
 
 
-def attend_back(starts, q, d_o, kva):
+def rear(
+    starts,
+    d_h2,
+    r1,
+    dy,
+    x,
+    q,
+    raw,
+    kva,
+    w_qkv,
+    w_out,
+    gsum,
+    g_attn,
+    g_ffn,
+    q_gain,
+    k_gain,
+    cosine,
+    sine,
+):
+    count, width = x.shape
+    q_cols = HEADS * HD
+    kv_cols = 2 * KV * HD
     vmem_spec = pl.BlockSpec(memory_space=pltpu.VMEM)
-    columns = kva.shape[3]
+    any_spec = pl.BlockSpec(memory_space=pl.ANY)
     return pl.pallas_call(
-        attend_back_kernel,
+        rear_kernel,
         out_shape=(
-            jax.ShapeDtypeStruct(q.shape, bf16),
-            jax.ShapeDtypeStruct((2, BLOCK, columns), bf16),
+            jax.ShapeDtypeStruct((count, width), bf16),
+            jax.ShapeDtypeStruct((count, q_cols + kv_cols), bf16),
+            jax.ShapeDtypeStruct((count, width), bf16),
+            jax.ShapeDtypeStruct((1, width), f32),
+            jax.ShapeDtypeStruct((1, width), f32),
+            jax.ShapeDtypeStruct((1, GROUP_COLS), f32),
+            jax.ShapeDtypeStruct((1, GROUP_COLS), f32),
+            jax.ShapeDtypeStruct(gsum.shape, bf16),
         ),
         in_specs=[
             pl.BlockSpec(memory_space=pltpu.SMEM),
-            vmem_spec,
-            vmem_spec,
-            pl.BlockSpec(memory_space=pl.ANY),
+            *[vmem_spec] * 6,
+            *[any_spec] * 4,
+            *[vmem_spec] * 6,
         ],
-        out_specs=(vmem_spec, vmem_spec),
+        out_specs=(*[vmem_spec] * 7, any_spec),
         scratch_shapes=[
-            pltpu.VMEM((8, 4, BLOCK, columns), bf16),
-            pltpu.VMEM((8, 4, BLOCK, columns), bf16),
+            pltpu.VMEM((width, q_cols + kv_cols), bf16),
+            pltpu.VMEM((q_cols, width), bf16),
+            pltpu.VMEM((8, 4, BLOCK, kv_cols), bf16),
+            pltpu.VMEM(gsum.shape, bf16),
+            pltpu.VMEM(gsum.shape, bf16),
+            pltpu.VMEM((2, gsum.shape[1] // 2, gsum.shape[2]), bf16),
+            pltpu.VMEM((2, *gsum.shape[1:]), bf16),
+            pltpu.VMEM((8, 4, BLOCK, kv_cols), bf16),
             pltpu.VMEM((2, BLOCK, 16 * BLOCK), f32),
-            *sum_landings(columns),
-            pltpu.SemaphoreType.DMA((16,)),
-            pltpu.SemaphoreType.DMA((16,)),
-            pltpu.SemaphoreType.DMA,
+            pltpu.VMEM((count, width), f32),
+            pltpu.VMEM((count, q_cols), bf16),
+            pltpu.VMEM((count, q_cols), bf16),
+            pltpu.VMEM((count, width), f32),
+            *sum_landings(kv_cols),
+            pltpu.SemaphoreType.DMA((24,)),
+            pltpu.SemaphoreType.DMA((24,)),
+            pltpu.SemaphoreType.DMA((5,)),
         ],
         compiler_params=pltpu.CompilerParams(
             collective_id=3, has_side_effects=True, vmem_limit_bytes=VMEM_BYTES
         ),
-        name="attend_back",
-    )(starts, q, d_o, kva)
+        name="rear",
+    )(
+        starts,
+        d_h2,
+        r1,
+        dy,
+        x,
+        q,
+        raw,
+        kva,
+        w_qkv,
+        w_out,
+        gsum,
+        g_attn,
+        g_ffn,
+        q_gain,
+        k_gain,
+        cosine,
+        sine,
+    )
 
 
 AXIS_ORDERS = (("dp_0", "seq", "head"), ("seq", "head", "dp_0"), ("head", "dp_0", "seq"))
 CHIP_AXES = ("dp_0", "seq", "head")
 
 
-class RingSum:
-    def __init__(self, copies, base, axis, part, half_land, full_land):
-        self.c = copies
-        self.base = base
-        self.axis = axis
-        self.part = part
-        self.hl = half_land
-        self.fl = full_land
-        self.i = lax.axis_index(axis)
-
-    def step1(self):
-        far = self.part.at[shift(self.i, 2)]
-        self.a = self.c.start(self.base, far.at[pl.ds(0, 2)], self.hl.at[0], self.axis, 1)
-        self.b = self.c.start(self.base + 1, far.at[pl.ds(2, 2)], self.hl.at[1], self.axis, -1)
-
-    def step2(self):
-        for copy, by, side in ((self.a, 1, 0), (self.b, -1, 1)):
-            copy.wait_recv()
-            block = self.part.at[shift(self.i, by)]
-            half = block.at[pl.ds(2 * side, 2)]
-            half[...] = (half[...].astype(f32) + self.hl[side].astype(f32)).astype(bf16)
-            new = self.c.start(self.base + 2 + side, block, self.fl.at[side], self.axis, by)
-            if side == 0:
-                self.a = new
-            else:
-                self.b = new
-
-    def finish(self):
-        self.a.wait_recv()
-        self.b.wait_recv()
-        own = self.part.at[self.i]
-        own[...] = (
-            own[...].astype(f32) + self.fl[0].astype(f32) + self.fl[1].astype(f32)
-        ).astype(bf16)
-        return own
-
-
 def projections_kernel(
-    h1_ref, da_ref, dqkv_ref, mix_ref, gain_ref, out_ref, gain_out, *scratch
+    h1_ref,
+    da_ref,
+    dqkv_ref,
+    mix_ref,
+    gain_ref,
+    gall_ref,
+    left_ref,
+    right_ref,
+    gain_out,
+    gboth_ref,
+    *scratch,
 ):
-    (h1c, dac, dqc, mxc, gsum) = scratch[:5]
-    parts = scratch[5:8]
-    half1, full1, half2, full2, last = (scratch[8 + 3 * k : 11 + 3 * k] for k in range(5))
-    send, recv = scratch[23:]
+    (h1c, dac, dqc, mxc, gsum, gboth) = scratch[:6]
+    parts = scratch[6:9]
+    half1, full1, half2, full2, last = (scratch[9 + 3 * k : 12 + 3 * k] for k in range(5))
+    send, recv, lsem = scratch[24:]
     tokens = h1_ref.shape[0]
     copies = Copies(send, recv)
     barrier = pltpu.get_barrier_semaphore()
@@ -664,19 +1103,7 @@
     pl.semaphore_signal(barrier, inc=1, device_id={"dp_1": other}, device_id_type=MESH)
     pl.semaphore_wait(barrier, 10)
 
-    def to_other(slot, src, dst):
-        copy = pltpu.make_async_remote_copy(
-            src_ref=src,
-            dst_ref=dst,
-            send_sem=send.at[slot],
-            recv_sem=recv.at[slot],
-            device_id={"dp_1": other},
-            device_id_type=MESH,
-        )
-        copy.start()
-        copies.started.append(copy)
-        return copy
-
+    to_other = copies.start_to_core
     mine, theirs = pl.ds(0, tokens), pl.ds(tokens, tokens)
 
     def piece(z, which):
@@ -691,6 +1118,11 @@
         moves.append(to_other(2 + 2 * z, h1_ref.at[:, piece(z, other)], h1c.at[theirs, cols]))
         moves.append(to_other(3 + 2 * z, da_ref.at[:, piece(z, other)], dac.at[theirs, cols]))
     gain_move = to_other(10, gain_ref, gsum.at[3, core])
+    grows = gall_ref.shape[1]
+    place = gboth.at[:, pl.ds(pl.multiple_of(core * grows, 16), grows)]
+    gmove = to_other(53, gall_ref, place)
+    gload = pltpu.make_async_copy(gall_ref, place, lsem.at[0])
+    gload.start()
     for z in range(4):
         cols = pl.ds(z * 256, 256)
         h1c[mine, cols] = h1_ref[:, piece(z, core)]
@@ -701,7 +1133,9 @@
         move.wait_recv()
 
     widths = [part.shape[4] for part in parts]
-    split = dqkv_ref.shape[1] - widths[0]
+    qkv_width = dqkv_ref.shape[1]
+    columns = qkv_width + mix_ref.shape[1]
+    split = qkv_width - widths[0]
     sources = (
         ((h1c, dqc, 0, widths[0], 0),),
         ((h1c, dqc, widths[0], split, 0), (dac, mxc, 0, widths[1] - split, split)),
@@ -745,6 +1179,10 @@
     ]
     for ring in rings:
         ring.step1()
+    gmove.wait_recv()
+    gload.wait()
+    gkeep = pltpu.make_async_copy(gboth, gboth_ref, lsem.at[1])
+    gkeep.start()
     gain_move.wait_recv()
     gsum[3, core] = gain_ref[...]
     total = gsum[3, 0] + gsum[3, 1]
@@ -782,15 +1220,20 @@
         value = owns[k][i].astype(f32)
         for n in range(3):
             value = value + last[k][n].astype(f32)
-        out_ref[:, place : place + widths[k]] = value
+        for ref, first, last_col in ((left_ref, 0, qkv_width), (right_ref, qkv_width, columns)):
+            low, high = max(first, place), min(last_col, place + widths[k])
+            if low < high:
+                ref[:, low - first : high - first] = value[:, low - place : high - place]
         place += widths[k]
+    gkeep.wait()
     copies.finish()
 
 
-def projections(h1, d_attn, d_qkv, mixed, gains):
+def projections(h1, d_attn, d_qkv, mixed, gains, gall):
     tokens, qkv_width = d_qkv.shape
     columns = qkv_width + mixed.shape[1]
     widths = (1536, 1536, columns - 3072)
+    any_spec = pl.BlockSpec(memory_space=pl.ANY)
     vmem_spec = pl.BlockSpec(memory_space=pltpu.VMEM)
     rows = h1.shape[1] // 2
 
@@ -800,54 +1243,69 @@
     return pl.pallas_call(
         projections_kernel,
         out_shape=(
-            jax.ShapeDtypeStruct((16, columns), f32),
+            jax.ShapeDtypeStruct((16, qkv_width), f32),
+            jax.ShapeDtypeStruct((16, mixed.shape[1]), f32),
             jax.ShapeDtypeStruct(gains.shape, f32),
+            jax.ShapeDtypeStruct((gall.shape[0], 2 * gall.shape[1], gall.shape[2]), bf16),
         ),
-        in_specs=[vmem_spec] * 5,
-        out_specs=(vmem_spec, vmem_spec),
+        in_specs=[*[vmem_spec] * 5, any_spec],
+        out_specs=(vmem_spec, vmem_spec, vmem_spec, any_spec),
         scratch_shapes=[
             pltpu.VMEM((2 * tokens, rows), bf16),
             pltpu.VMEM((2 * tokens, rows), bf16),
             pltpu.VMEM((2 * tokens, qkv_width), bf16),
             pltpu.VMEM((2 * tokens, mixed.shape[1]), bf16),
             pltpu.VMEM((4, 4, *gains.shape), f32),
+            pltpu.VMEM((gall.shape[0], 2 * gall.shape[1], gall.shape[2]), bf16),
             *each(lambda w: (4, 4, 4, 16, w)),
             *each(lambda w: (2, 2, 4, 16, w)),
             *each(lambda w: (2, 4, 4, 16, w)),
             *each(lambda w: (2, 2, 16, w)),
             *each(lambda w: (2, 4, 16, w)),
             *each(lambda w: (3, 16, w)),
-            pltpu.SemaphoreType.DMA((53,)),
-            pltpu.SemaphoreType.DMA((53,)),
+            pltpu.SemaphoreType.DMA((54,)),
+            pltpu.SemaphoreType.DMA((54,)),
+            pltpu.SemaphoreType.DMA((2,)),
         ],
         compiler_params=pltpu.CompilerParams(
             collective_id=4, has_side_effects=True, vmem_limit_bytes=VMEM_BYTES
         ),
         name="projections",
-    )(h1, d_attn, d_qkv, mixed, gains)
-
-
-def rms_parts(v):
-    inverse = lax.rsqrt(jnp.mean(v * v, axis=-1, keepdims=True) + EPS)
-    return (v * inverse, inverse)
-
-
-def rms_back(grad, normed, inverse):
-    return inverse * (grad - normed * jnp.mean(grad * normed, axis=-1, keepdims=True))
-
-
-def rotate(v, cosine, sine):
-    half = v.shape[-1] // 2
-    first = v[..., :half]
-    second = v[..., half:]
-    return jnp.concatenate([first * cosine - second * sine, second * cosine + first * sine], -1)
-
-
-def angle_tables(positions, width):
-    half = width // 2
-    freq = jnp.exp(jnp.arange(half, dtype=f32) * (-2.0 * math.log(10000.0) / width))
+    )(h1, d_attn, d_qkv, mixed, gains, gall)
+
+
+def widen_kernel(g_ref, gin_ref, gdn_ref):
+    units = gdn_ref.shape[0]
+    gin_ref[:, 0, :] = g_ref[:units].astype(f32)
+    gin_ref[:, 1, :] = g_ref[units : 2 * units].astype(f32)
+    gdn_ref[...] = g_ref[2 * units :].astype(f32)
+
+
+def widen(g, units):
+    tiles, _, tile = g.shape
+    return pl.pallas_call(
+        widen_kernel,
+        grid=(tiles,),
+        out_shape=(
+            jax.ShapeDtypeStruct((units, 2, tiles * tile), f32),
+            jax.ShapeDtypeStruct((units, tiles * tile), f32),
+        ),
+        in_specs=[pl.BlockSpec((None, 3 * units, tile), lambda n: (n, 0, 0))],
+        out_specs=(
+            pl.BlockSpec((units, 2, tile), lambda n: (0, 0, n)),
+            pl.BlockSpec((units, tile), lambda n: (0, n)),
+        ),
+        compiler_params=pltpu.CompilerParams(vmem_limit_bytes=VMEM_BYTES),
+        name="widen",
+    )(g)
+
+
+def angle_tables(positions, columns):
+    lane = jnp.arange(columns)
+    freq = jnp.exp((lane % (HD // 2)).astype(f32) * (-2.0 * math.log(10000.0) / HD))
     angle = positions.astype(f32)[:, None] * freq[None, :]
-    return (jnp.cos(angle), jnp.sin(angle))
+    sign = jnp.where(lane % HD < HD // 2, -1.0, 1.0)
+    return (jnp.cos(angle), jnp.sin(angle) * sign[None, :])
 
 
 def body(
@@ -857,91 +1315,58 @@
     count = rows * tok
     n_seq = lax.axis_size("seq")
     n_head = lax.axis_size("head")
-    span = tok * n_head
-    seq_index = lax.axis_index("seq")
-    head_index = lax.axis_index("head")
-    tok_pos = seq_index * span + head_index * tok + jnp.arange(tok)
-    cosine, sine = angle_tables(tok_pos, HD)
-    cosine = cosine[None, :, None, :]
-    sine = sine[None, :, None, :]
-    dy_all = lax.all_gather(d_out[None], ("seq", "head"), axis=0, tiled=True)
-    dy_all = dy_all.reshape(n_seq, n_head, rows, tok, width)
-    w_in = w_ffn_in.transpose(1, 0, 2).reshape(-1, width)
-    xf = tokens.reshape(count, width).astype(f32)
-    dy = d_out.reshape(count, width).astype(f32)
-    n1, inv1 = rms_parts(xf)
-    h1 = (n1 * g_attn).astype(bf16)
-    qkv = jnp.dot(h1, w_qkv, preferred_element_type=f32)
-    q_raw = qkv[..., : HEADS * HD].reshape(rows, tok, HEADS, HD)
-    k_raw = qkv[..., HEADS * HD : (HEADS + KV) * HD].reshape(rows, tok, KV, HD)
-    v_raw = qkv[..., (HEADS + KV) * HD :].reshape(rows, tok, KV, HD)
-    q_normed, inv_q = rms_parts(q_raw)
-    k_normed, inv_k = rms_parts(k_raw)
-    q_rot = rotate(q_normed * q_gain, cosine, sine).astype(bf16).reshape(count, HEADS * HD)
-    k_rot = rotate(k_normed * k_gain, cosine, sine)
-    kv = jnp.concatenate([k_rot, v_raw], -1).astype(bf16).reshape(rows, tok, KV * 2 * HD)
-    mixed, kva = attend(doc_starts, q_rot, kv)
-    attn = jnp.dot(mixed, w_out, preferred_element_type=f32)
-    r1 = xf + attn
-    n2, inv2 = rms_parts(r1)
-    h2 = (n2 * g_ffn).astype(bf16)
-    outp, d_h2, grad_in, grad_down = ffn(h2.reshape(rows, tok, width), dy_all, w_in, w_ffn_out)
-    d_h2 = d_h2.reshape(count, width)
+    first = (lax.axis_index("seq") * n_head + lax.axis_index("head")) * tok
+    cosine, sine = angle_tables(first + jnp.arange(count) % tok, GROUP_COLS)
+    x = tokens.reshape(count, width)
+    dy = d_out.reshape(count, width)
+    ga = g_attn[None]
+    gf = g_ffn[None]
+    qg = jnp.tile(q_gain, PER_GROUP)[None]
+    kg = jnp.tile(k_gain, PER_GROUP)[None]
+    h1, raw, q, kva, mixed, r1, h2, dy_all = front(
+        doc_starts, x, w_qkv, w_out, ga, gf, qg, kg, cosine, sine, d_out
+    )
+    outp, d_h2, gsum = ffn(h2.reshape(rows, tok, width), dy_all, w_ffn_in, w_ffn_out)
     ffn_sum = lax.psum_scatter(
         outp.reshape(n_seq * n_head * count, width), ("seq", "head"), scatter_dimension=0, tiled=True
     )
-    grad_in_sum, grad_down_sum = (
-        lax.psum(grad_in, DP).astype(f32),
-        lax.psum(grad_down, DP).astype(f32),
+    d_attn, d_qkv, grad_x, grad_gattn, grad_gffn, grad_qgain, grad_kgain, gall = rear(
+        doc_starts,
+        d_h2.reshape(count, width),
+        r1,
+        dy,
+        x,
+        q,
+        raw,
+        kva,
+        w_qkv,
+        w_out,
+        gsum,
+        ga,
+        gf,
+        qg,
+        kg,
+        cosine,
+        sine,
     )
-    grad_in_sum = grad_in_sum.reshape(2, -1, width).transpose(1, 0, 2)
-    grad_gffn = jnp.sum(d_h2 * n2, axis=0)
-    d_r1 = dy + rms_back(d_h2 * g_ffn, n2, inv2)
-    d_attn = d_r1.astype(bf16)
-    d_o = lax.dot_general(
-        d_attn, w_out, (((1,), (1,)), ((), ())), preferred_element_type=f32
-    ).astype(bf16)
-    d_q, d_kv = attend_back(doc_starts, q_rot, d_o, kva)
-    d_qrot = d_q.reshape(rows, tok, HEADS, HD).astype(f32)
-    d_kv = d_kv.reshape(rows, tok, KV, 2 * HD)
-    d_krot = d_kv[..., :HD].astype(f32)
-    d_vraw = d_kv[..., HD:]
-    d_qs = rotate(d_qrot, cosine, -sine)
-    d_ks = rotate(d_krot, cosine, -sine)
-    grad_qgain = jnp.sum(d_qs * q_normed, axis=(0, 1, 2))
-    grad_kgain = jnp.sum(d_ks * k_normed, axis=(0, 1, 2))
-    d_qraw = rms_back(d_qs * q_gain, q_normed, inv_q)
-    d_kraw = rms_back(d_ks * k_gain, k_normed, inv_k)
-    d_qkv = jnp.concatenate(
-        [
-            d_qraw.astype(bf16).reshape(count, HEADS * HD),
-            d_kraw.astype(bf16).reshape(count, KV * HD),
-            d_vraw.reshape(count, KV * HD),
-        ],
-        -1,
-    )
-    d_h1 = lax.dot_general(
-        d_qkv, w_qkv, (((1,), (1,)), ((), ())), preferred_element_type=f32
-    )
-    grad_gattn = jnp.sum(d_h1 * n1, axis=0)
-    grad_x = (d_r1 + rms_back(d_h1 * g_attn, n1, inv1)).astype(bf16)
-    gains = jnp.concatenate([grad_gattn, grad_gffn, grad_qgain, grad_kgain])
+    gains = jnp.concatenate([grad_gattn, grad_gffn, grad_qgain, grad_kgain], 1)[0]
     gains = jnp.pad(gains, (0, 40 * 128 - gains.shape[0])).reshape(40, 128)
-    weight_part, gains = projections(h1, d_attn, d_qkv, mixed, gains)
+    grad_qkv, grad_out, gains, gboth = projections(h1, d_attn, d_qkv, mixed, gains, gall)
+    grad_in, grad_down = widen(gboth, w_ffn_out.shape[0])
     gains = gains.reshape(-1)
     output = (r1 + ffn_sum.astype(f32)).astype(bf16)
-    qkv_width = w_qkv.shape[1]
+    heads = gains[2 * width : 2 * width + 2 * GROUP_COLS].reshape(2, PER_GROUP, HD).sum(1)
     return (
         output.reshape(rows, tok, width),
         grad_x.reshape(rows, tok, width),
-        weight_part[:, :qkv_width],
-        weight_part[:, qkv_width:].T,
-        grad_in_sum,
-        grad_down_sum,
+        grad_qkv,
+        grad_out.T,
+        grad_in,
+        grad_down,
         gains[:width],
         gains[width : 2 * width],
-        gains[2 * width : 2 * width + HD],
-        gains[2 * width + HD : 2 * width + 2 * HD],
+        heads[0],
+        heads[1],
     )
 
 

time: 443 us -> 370 us (0.84)
  local copies, waits for them, and re-layouts: 72.1 us -> 7.31 us
  Pallas kernels: 275 us -> 338 us
  other arithmetic: 43 us -> 4 us
  matrix products: 26.7 us -> 0 us
  waiting for transfers between devices: 6.67 us -> 0.02 us
    pallas_call x3 -> x4, Pallas kernels: 168 us -> 231 us  [the longest x1 83.9 us: rear(): pl.pallas_call(rear_kernel, out_shape=(jax.ShapeDtypeStruct((count, width...]
    dot_general x4 -> x0, matrix products: 26.7 us -> none  [the longest x1 9.43 us: body(): lax.dot_general(d_qkv, w_qkv, (((1,), (1,)), ((), ())), preferred_element...]
    mul x16 -> x0, local copies, waits for them, and re-layouts: 22.4 us -> none  [the longest x6 12.1 us: rms_parts(): return (v * inverse, inverse)]
    reshape x6 -> x1, local copies, waits for them, and re-layouts: 11.2 us -> 0.08 us  [body(): gains[2 * width:2 * width + 2 * GROUP_COLS].reshape(2, PER_GROUP, HD).sum(1)]
    concatenate x6 -> x0, local copies, waits for them, and re-layouts: 10.9 us -> none  [the longest x4 9.49 us: rotate(): jnp.concatenate([first * cosine - second * sine, second * cosine + first...]
    reduce_sum x8 -> x1, other arithmetic: 9.97 us -> 0.02 us  [body(): gains[2 * width:2 * width + 2 * GROUP_COLS].reshape(2, PER_GROUP, HD).sum(1)]
    transpose x1 -> x0, other arithmetic: 9.4 us -> none  [body(): grad_in_sum = grad_in_sum.reshape(2, -1, width).transpose(1, 0, 2)]
    convert_element_type x6 -> x1, other arithmetic: 10.4 us -> 1.94 us  [body(): output = (r1 + ffn_sum.astype(f32)).astype(bf16)]
  transfers between devices with their start and end apart: 3 -> 1, of which waited for: 1 -> 0; matrix products, arithmetic and copies ran while one was open for 30% -> 1% of each run, Pallas kernels for 38% -> 43%
where the time goes in v2:
time: 370 us; the launch traced here: 364 us
  Pallas kernels  338 us (91%)
  between operations  14.3 us (4%)
  local copies, waits for them, and re-layouts  7.31 us (2%)
  other arithmetic  4 us (1%)
    pallas_call x1, Pallas kernels, ffn(): pl.pallas_call(ffn_kernel, out_shape=(jax.ShapeDtypeStruct((4, 4, 2, BLOC...  107 us
    pallas_call x1, Pallas kernels, rear(): pl.pallas_call(rear_kernel, out_shape=(jax.ShapeDtypeStruct((count, width...  83.9 us
    pallas_call x1, Pallas kernels, front(): pl.pallas_call(front_kernel, out_shape=(jax.ShapeDtypeStruct((count, widt...  76.5 us
    pallas_call x1, Pallas kernels, projections(): pl.pallas_call(projections_kernel, out_shape=(jax.ShapeDtypeStruct((16, q...  63.5 us
    pallas_call x1, Pallas kernels, widen(): pl.pallas_call(widen_kernel, grid=(tiles,), out_shape=(jax.ShapeDtypeStru...  7.53 us
  transfers between devices with their start and end apart: 1, of which 0 were waited for; matrix products, arithmetic and copies ran while one was open for 1% of the time, Pallas kernels for 43%

profile of v2, /device:TPU:0, one launch (start us, length us, event | category | flops | bytes accessed | tf_op | source)
XLA Modules:
  0.0 363.8 jit_solution(16217244214129427620)
XLA Ops:
  7.2 0.0 reduce-scatter.2.cloned.1.call-start
  7.3 0.7 tile.4
  7.9 0.6 broadcast_in_dim_tile.6.qg_ref
  8.6 0.7 tile.5
  9.2 0.6 broadcast_in_dim_tile.7.kg_ref
  9.9 1.2 fusion
  11.1 76.5 %front.1 = (bf16[128,2048]{1,0:T(8,128)(2,1)}, f32[128,2688]{1,0:T(8,128)}, bf16[128,1792]{1,0:T(8,128)(2,1)}, bf16[8,4,64,896]{3,2,1,0:T(8,128)(2,1)}, bf16[128...) custom-call(s32[2,4]{1,0:T(2,128)} %starts_ref.3, ...), custom_call_target="tpu_custom_call" | custom-call | tf_op jit(solution)/shard_map/front/pallas_call | solution.py:760
  87.6 106.8 %ffn.1 = (bf16[4,4,2,64,2048]{4,3,2,1,0:T(8,128)(2,1)}, f32[2,64,2048]{2,1,0:T(8,128)}, bf16[4,672,512]{2,1,0:T(8,128)(2,1)}) custom-call(bf16[2,64,2048]{2,1,0:T(8,128)(2,1)} %bitcast.25, bf16[8,4,64,2048]{3,2,1,0:T(8,128)(2,1)} %get-tuple-element.37.dy_ref, bf16[448,2,2048]{2,1,0:T(2,128)(2,1)} %win_ref.1, bf16[448,2048]{1,0:T(8,128)(2,1)} %wdn_ref.1), custom_call_target="tpu_custom_call" | custom-call | tf_op jit(solution)/shard_map/ffn/pallas_call | solution.py:467
  194.4 0.0 reduce-scatter.2.cloned.1.call-update
  194.4 83.9 %rear.1 = (bf16[128,2048]{1,0:T(8,128)(2,1)}, bf16[128,2688]{1,0:T(8,128)(2,1)}, bf16[128,2048]{1,0:T(8,128)(2,1)}, f32[1,2048]{1,0:T(1,128)}, f32[1,2048]{1,0:T...) custom-call(s32[2,4]{1,0:T(2,128)} %starts_ref.3, f32[128,2048]{1,0:T(8,128)} %bitcast.24, ...), custom_call_target="tpu_custom_call" | custom-call | tf_op jit(solution)/shard_map/rear/pallas_call | solution.py:1006
  278.3 0.8 maximum_reduce_fusion
  279.1 0.6 pad_bitcast_fusion.gain_ref
  279.7 63.5 %projections.1 = (f32[16,2688]{1,0:T(8,128)}, f32[16,1792]{1,0:T(8,128)}, f32[40,128]{1,0:T(8,128)}, bf16[4,1344,512]{2,1,0:T(8,128)(2,1)}) custom-call(bf16[128,2048]{1,0:T(8,128)(2,1)} %get-tuple-element.45.h1_ref, bf16[128,2048]{1,0:T(8,128)(2,1)} %get-tuple-element.46.da_ref, bf16[128,2688]{1,0:T(8,128)(2,1)} %get-tuple-element.47.dqkv_ref, ...), custom_call_target="tpu_custom_call" | custom-call | tf_op jit(solution)/shard_map/projections/pallas_call | solution.py:1243
  343.2 0.0 copy-start.4
  343.2 0.0 copy-start
  343.2 0.8 slice.26
  343.9 0.1 reshape.96
  344.0 0.0 copy-start.1
  344.0 0.0 copy-start.2
  344.0 0.0 copy-start.3
  344.0 7.5 %widen.1 = (f32[448,2,2048]{2,1,0:T(2,128)}, f32[448,2048]{1,0:T(8,128)}) custom-call(bf16[4,1344,512]{2,1,0:T(8,128)(2,1)} %get-tuple-element.56.g_ref), custom_call_target="tpu_custom_call" | custom-call | tf_op jit(solution)/shard_map/widen/pallas_call | solution.py:1286
  351.6 0.5 slice_bitcast_fusion.2
  352.1 0.0 copy-done.4
  352.1 0.6 slice_bitcast_fusion
  352.7 0.0 copy-done
  352.7 1.9 add_convert_fusion
  354.6 0.0 copy-done.1
  354.6 0.8 copy.24
  355.4 0.0 copy-done.2
  355.4 0.7 copy.25
  356.1 0.0 copy-done.3
  356.1 0.6 copy.26
  (4 shorter events, 0.0 us)
Async XLA Ops:
  7.2 345.5 %reduce-scatter.2.cloned.1.call-start = ((), (), s32[]{:S(2)}) async-start(), calls=%async_computation.1 | async-start | bytes 8912896 | tf_op jit(solution)/shard_map/reduce_scatter | solution.py:1330
  343.2 8.9 %copy-start.4 = (f32[40,128]{1,0:T(8,128)S(1)}, f32[40,128]{1,0:T(8,128)}, u32[]{:S(2)}) copy-start(f32[40,128]{1,0:T(8,128)} %get-tuple-element.59) | copy-start | bytes 61444
  343.2 9.5 %copy-start = (f32[128,2048]{1,0:T(8,128)S(1)}, f32[128,2048]{1,0:T(8,128)}, u32[]{:S(2)}) copy-start(f32[128,2048]{1,0:T(8,128)} %get-tuple-element.35.r1_ref) | copy-start | bytes 3145732
  344.0 10.6 %copy-start.1 = (bf16[128,2048]{1,0:T(8,128)(2,1)S(1)}, bf16[128,2048]{1,0:T(8,128)(2,1)}, u32[]{:S(2)}) copy-start(bf16[128,2048]{1,0:T(8,128)(2,1)} %get-tuple-element.44) | copy-start | bytes 1572868
  344.0 11.4 %copy-start.2 = (f32[16,2688]{1,0:T(8,128)S(1)}, f32[16,2688]{1,0:T(8,128)}, u32[]{:S(2)}) copy-start(f32[16,2688]{1,0:T(8,128)} %get-tuple-element.80) | copy-start | bytes 516100
  344.0 12.1 %copy-start.3 = (f32[16,1792]{1,0:T(8,128)S(1)}, f32[16,1792]{1,0:T(8,128)}, u32[]{:S(2)}) copy-start(f32[16,1792]{1,0:T(8,128)} %get-tuple-element.55) | copy-start | bytes 344068
Sparse Core Ops, SparseCore 0:
  194.5 95.4 reduce-scatter.1

commit v3 on v2

--- a/solution.py
+++ b/solution.py
@@ -150,7 +150,7 @@
 class PlaneSum:
     def __init__(self, copies, base, half, part, land1, land2, land3, land4):
         self.c = copies
-        self.base = base + 8 * half
+        self.base = base + 12 * half
         self.half = half
         self.part = part
         self.l1, self.l2, self.l3, self.l4 = (
@@ -165,49 +165,70 @@
     def add(self, ref, other):
         ref[...] = (ref[...].astype(f32) + other[...].astype(f32)).astype(ref.dtype)
 
-    def step1(self):
+    def far(self):
         ax = GROUP[self.half]
         row = self.row(2)
         self.a = self.c.start(self.base, self.part.at[row, pl.ds(0, 2)], self.l1.at[0], ax, 1)
         self.b = self.c.start(self.base + 1, self.part.at[row, pl.ds(2, 2)], self.l1.at[1], ax, -1)
 
-    def step2(self):
+    def early(self):
         ax = GROUP[self.half]
+        one, two = pl.ds(0, 2), pl.ds(2, 2)
+        right, left = self.part.at[self.row(1)], self.part.at[self.row(-1)]
+        self.ea = self.c.start(self.base + 2, right.at[two], self.l2.at[0, two], ax, 1)
+        self.eb = self.c.start(self.base + 3, left.at[one], self.l2.at[1, one], ax, -1)
+
+    def late(self):
+        ax = GROUP[self.half]
+        one, two = pl.ds(0, 2), pl.ds(2, 2)
+        right, left = self.part.at[self.row(1), one], self.part.at[self.row(-1), two]
         self.a.wait_recv()
-        self.add(self.part.at[self.row(1), pl.ds(0, 2)], self.l1.at[0])
-        self.a = self.c.start(self.base + 2, self.part.at[self.row(1)], self.l2.at[0], ax, 1)
+        self.add(right, self.l1.at[0])
+        self.a = self.c.start(self.base + 4, right, self.l2.at[0, one], ax, 1)
         self.b.wait_recv()
-        self.add(self.part.at[self.row(-1), pl.ds(2, 2)], self.l1.at[1])
-        self.b = self.c.start(self.base + 3, self.part.at[self.row(-1)], self.l2.at[1], ax, -1)
-
-    def step3(self):
+        self.add(left, self.l1.at[1])
+        self.b = self.c.start(self.base + 5, left, self.l2.at[1, two], ax, -1)
+
+    def inner_start(self):
         ax = INNER[self.half]
         n = self.part.shape[2] // 2
-        self.a.wait_recv()
-        self.b.wait_recv()
+        one, two = pl.ds(0, n), pl.ds(n, n)
+        for copy in (self.ea, self.eb, self.a, self.b):
+            copy.wait_recv()
         rows = self.part.at[self.row()]
-        rows[...] = (
-            rows[...].astype(f32) + self.l2[0].astype(f32) + self.l2[1].astype(f32)
-        ).astype(rows.dtype)
-        block = self.part.at[self.row(), shift(self.i, 2)]
-        self.a = self.c.start(self.base + 4, block.at[pl.ds(0, n)], self.l3.at[0], ax, 1)
-        self.b = self.c.start(self.base + 5, block.at[pl.ds(n, n)], self.l3.at[1], ax, -1)
-
-    def step4(self):
+
+        def sum_of(k):
+            rows[k] = (
+                rows[k].astype(f32) + self.l2[0, k].astype(f32) + self.l2[1, k].astype(f32)
+            ).astype(rows.dtype)
+
+        sum_of(shift(self.i, 2))
+        block = rows.at[shift(self.i, 2)]
+        self.a = self.c.start(self.base + 6, block.at[one], self.l3.at[0], ax, 1)
+        self.b = self.c.start(self.base + 7, block.at[two], self.l3.at[1], ax, -1)
+        sum_of(shift(self.i, 1))
+        sum_of(shift(self.i, -1))
+        right, left = rows.at[shift(self.i, 1)], rows.at[shift(self.i, -1)]
+        self.ea = self.c.start(self.base + 8, right.at[two], self.l4.at[0, two], ax, 1)
+        self.eb = self.c.start(self.base + 9, left.at[one], self.l4.at[1, one], ax, -1)
+        sum_of(self.i)
+
+    def inner_late(self):
         ax = INNER[self.half]
         n = self.part.shape[2] // 2
+        one, two = pl.ds(0, n), pl.ds(n, n)
+        right = self.part.at[self.row(), shift(self.i, 1), one]
+        left = self.part.at[self.row(), shift(self.i, -1), two]
         self.a.wait_recv()
-        right = self.part.at[self.row(), shift(self.i, 1)]
-        self.add(right.at[pl.ds(0, n)], self.l3.at[0])
-        self.a = self.c.start(self.base + 6, right, self.l4.at[0], ax, 1)
+        self.add(right, self.l3.at[0])
+        self.a = self.c.start(self.base + 10, right, self.l4.at[0, one], ax, 1)
         self.b.wait_recv()
-        left = self.part.at[self.row(), shift(self.i, -1)]
-        self.add(left.at[pl.ds(n, n)], self.l3.at[1])
-        self.b = self.c.start(self.base + 7, left, self.l4.at[1], ax, -1)
+        self.add(left, self.l3.at[1])
+        self.b = self.c.start(self.base + 11, left, self.l4.at[1, two], ax, -1)
 
     def result(self):
-        self.a.wait_recv()
-        self.b.wait_recv()
+        for copy in (self.ea, self.eb, self.a, self.b):
+            copy.wait_recv()
         own = self.part[self.row(), self.i].astype(f32)
         return own + self.l4[0].astype(f32) + self.l4[1].astype(f32)
 
@@ -230,29 +251,31 @@
         self.hl = half_land
         self.fl = full_land
         self.i = lax.axis_index(axis)
-
-    def step1(self):
+        n = part.shape[1] // 2
+        self.one, self.two = pl.ds(0, n), pl.ds(n, n)
+
+    def start(self):
         far = self.part.at[shift(self.i, 2)]
-        n = far.shape[0] // 2
-        self.a = self.c.start(self.base, far.at[pl.ds(0, n)], self.hl.at[0], self.axis, 1)
-        self.b = self.c.start(self.base + 1, far.at[pl.ds(n, n)], self.hl.at[1], self.axis, -1)
-
-    def step2(self):
-        for copy, by, side in ((self.a, 1, 0), (self.b, -1, 1)):
+        right, left = self.part.at[shift(self.i, 1)], self.part.at[shift(self.i, -1)]
+        one, two, ax = self.one, self.two, self.axis
+        self.a = self.c.start(self.base, far.at[one], self.hl.at[0], ax, 1)
+        self.b = self.c.start(self.base + 1, far.at[two], self.hl.at[1], ax, -1)
+        self.ea = self.c.start(self.base + 2, right.at[two], self.fl.at[0, two], ax, 1)
+        self.eb = self.c.start(self.base + 3, left.at[one], self.fl.at[1, one], ax, -1)
+
+    def late(self):
+        right = self.part.at[shift(self.i, 1), self.one]
+        left = self.part.at[shift(self.i, -1), self.two]
+        self.a.wait_recv()
+        right[...] = (right[...].astype(f32) + self.hl[0].astype(f32)).astype(bf16)
+        self.a = self.c.start(self.base + 4, right, self.fl.at[0, self.one], self.axis, 1)
+        self.b.wait_recv()
+        left[...] = (left[...].astype(f32) + self.hl[1].astype(f32)).astype(bf16)
+        self.b = self.c.start(self.base + 5, left, self.fl.at[1, self.two], self.axis, -1)
+
+    def finish(self):
+        for copy in (self.ea, self.eb, self.a, self.b):
             copy.wait_recv()
-            block = self.part.at[shift(self.i, by)]
-            n = block.shape[0] // 2
-            half = block.at[pl.ds(n * side, n)]
-            half[...] = (half[...].astype(f32) + self.hl[side].astype(f32)).astype(bf16)
-            new = self.c.start(self.base + 2 + side, block, self.fl.at[side], self.axis, by)
-            if side == 0:
-                self.a = new
-            else:
-                self.b = new
-
-    def finish(self):
-        self.a.wait_recv()
-        self.b.wait_recv()
         own = self.part.at[self.i]
         own[...] = (
             own[...].astype(f32) + self.fl[0].astype(f32) + self.fl[1].astype(f32)
@@ -385,26 +408,23 @@
 
     @pl.loop(0, 4)
     def _(k):
-        forward(group(lax.div(k, 2), 1 - 2 * lax.rem(k, 2)))
+        q = group(lax.div(k, 2), 1 - 2 * lax.rem(k, 2))
+        forward(q)
+        back(q)
 
     for gather in gathers:
         gather.finish()
+    sums = [PlaneSum(copies, 16, half, dpt, l1, l2, l3, l4) for half in (0, 1)]
+    for total in sums:
+        total.early()
 
     @pl.loop(0, 2)
     def _(half):
         forward(group(half, 2))
         back(group(half, 2))
 
-    sums = [PlaneSum(copies, 16, half, dpt, l1, l2, l3, l4) for half in (0, 1)]
     for total in sums:
-        total.step1()
-
-    @pl.loop(0, 4)
-    def _(k):
-        back(group(lax.div(k, 2), 1 - 2 * lax.rem(k, 2)))
-
-    for total in sums:
-        total.step2()
+        total.far()
 
     @pl.loop(0, 2)
     def _(half):
@@ -421,16 +441,13 @@
         cols = pl.ds(n * tile, tile)
         gst[n, : 2 * units] = nn(dbo[...], h2a[:, :, :, cols].reshape(tokens, tile)).astype(bf16)
         gst[n, 2 * units :] = nn(hid[...], dya[:, :, :, cols].reshape(tokens, tile)).astype(bf16)
-        swaps.append(
-            copies.start_to_core(32 + n, gst.at[n, theirs], gland.at[n])
-        )
-    for total in sums:
-        total.step3()
+        swaps.append(copies.start_to_core(40 + n, gst.at[n, theirs], gland.at[n]))
+        if n == 2:
+            for total in sums:
+                total.late()
 
     def out_copy(q):
-        slot = q % 2
-        place = outp_ref.at[q, :, 0] if q < 4 else outp_ref.at[:, q - 4, 1]
-        return pltpu.make_async_copy(stage.at[slot], place, osem.at[slot])
+        return pltpu.make_async_copy(stage.at[q % 2], outp_ref.at[q], osem.at[q % 2])
 
     def out_part(q):
         if q >= 2:
@@ -439,12 +456,14 @@
         stage[q % 2] = value.astype(bf16).reshape(4, BLOCK, width)
         out_copy(q).start()
 
-    for q in range(4):
+    for q in range(6):
         out_part(q)
     for total in sums:
-        total.step4()
-    for q in range(4, 8):
+        total.inner_start()
+    for q in range(6, 8):
         out_part(q)
+    for total in sums:
+        total.inner_late()
     for half in (0, 1):
         dh2_ref[half] = sums[half].result()
     for n, swap in enumerate(swaps):
@@ -467,7 +486,7 @@
     return pl.pallas_call(
         ffn_kernel,
         out_shape=(
-            jax.ShapeDtypeStruct((4, 4, 2, BLOCK, width), bf16),
+            jax.ShapeDtypeStruct((8, 4, BLOCK, width), bf16),
             jax.ShapeDtypeStruct((2, BLOCK, width), f32),
             jax.ShapeDtypeStruct((width // tile, 3 * units // 2, tile), bf16),
         ),
@@ -486,8 +505,8 @@
             pltpu.VMEM((2, 4, BLOCK, width), bf16),
             pltpu.VMEM((width // tile, 3 * units, tile), bf16),
             pltpu.VMEM((width // tile, 3 * units // 2, tile), bf16),
-            pltpu.SemaphoreType.DMA((36,)),
-            pltpu.SemaphoreType.DMA((36,)),
+            pltpu.SemaphoreType.DMA((44,)),
+            pltpu.SemaphoreType.DMA((44,)),
             pltpu.SemaphoreType.DMA((5,)),
             pltpu.SemaphoreType.DMA((2,)),
         ],
@@ -816,76 +835,129 @@
     x_ref,
     q_ref,
     raw_ref,
+    h1_ref,
+    mix_ref,
     kva_ref,
     wqkv_ref,
     wout_ref,
     gsum_ref,
+    outp_ref,
     ga_ref,
     gf_ref,
     qg_ref,
     kg_ref,
     cos_ref,
     sin_ref,
-    da_ref,
-    dqkv_ref,
+    y_ref,
     gx_ref,
     gga_ref,
     ggf_ref,
     gq_ref,
     gk_ref,
     gall_ref,
-    wqkv,
-    wo,
+    h1_out,
+    da_out,
+    dq_out,
+    mx_out,
+    wbuf,
+    wkv,
     kva,
     gsum,
-    gfull,
     gl1,
     gl2,
-    part,
+    gboth,
+    outp,
     mask,
     d_r1,
     d_o,
     dq,
     d_h1,
-    l1,
-    l2,
-    l3,
-    l4,
-    send,
-    recv,
-    lsem,
+    da,
+    h1c,
+    dac,
+    dqc,
+    mxc,
+    *scratch,
 ):
+    landings, out_landings = scratch[:4], scratch[4:8]
+    send, recv, lsem = scratch[8:]
     count, width = x_ref.shape
     q_cols = HEADS * HD
     k_cols = KV * HD
+    seq, head = lax.axis_index("seq"), lax.axis_index("head")
+    far_rows = (shift(seq, 2), 4 + shift(head, 2))
     loads = [
-        pltpu.make_async_copy(wout_ref, wo, lsem.at[0]),
+        pltpu.make_async_copy(outp_ref.at[far_rows[0]], outp.at[far_rows[0]], lsem.at[5]),
+        pltpu.make_async_copy(outp_ref.at[far_rows[1]], outp.at[far_rows[1]], lsem.at[6]),
+        pltpu.make_async_copy(gsum_ref, gsum, lsem.at[3]),
+    ]
+    for half in (0, 1):
+        for by in (1, 3, 0):
+            row = 4 * half + shift(head if half else seq, by)
+            loads.append(
+                pltpu.make_async_copy(outp_ref.at[row], outp.at[row], lsem.at[7 + 4 * half + by])
+            )
+    loads += [
+        pltpu.make_async_copy(wout_ref, wbuf.at[pl.ds(0, q_cols)], lsem.at[0]),
         pltpu.make_async_copy(kva_ref, kva, lsem.at[1]),
-        pltpu.make_async_copy(wqkv_ref, wqkv, lsem.at[2]),
-        pltpu.make_async_copy(gsum_ref, gsum, lsem.at[3]),
+        pltpu.make_async_copy(wqkv_ref.at[:, pl.ds(q_cols, 2 * k_cols)], wkv, lsem.at[2]),
     ]
     for load in loads:
         load.start()
+    load_wo, load_kva, load_wkv = loads[-3:]
+    load_wq = pltpu.make_async_copy(
+        wqkv_ref.at[:, pl.ds(0, q_cols)], wbuf.at[:, pl.ds(0, q_cols)], lsem.at[5]
+    )
     copies = Copies(send, recv)
-    barrier_with(("dp_0", "seq", "head"))
-    gring = RingSum(copies, 16, "dp_0", gsum, gl1, gl2)
-    gback = RingGather(copies, 20, "dp_0", gfull)
-    loads[3].wait()
-    gring.step1()
+    core = lax.axis_index("dp_1")
+    mine, theirs = pl.ds(0, count), pl.ds(count, count)
+
+    def piece(z, which):
+        return pl.ds(pl.multiple_of(z * 512 + which * 256, 256), 256)
+
+    barrier_with(("dp_0", "seq", "head"), core=True)
+    outs = [PlaneSum(copies, 24, half, outp, *out_landings) for half in (0, 1)]
+    loads[0].wait()
+    outs[0].far()
+    loads[1].wait()
+    outs[1].far()
+    gring = RingSum(copies, 48, "dp_0", gsum, gl1, gl2)
+    grows = gsum.shape[1]
+    place = pl.ds(pl.multiple_of(core * grows, 16), grows)
+    gfull = gboth.at[:, place]
+    gback = RingGather(copies, 54, "dp_0", gfull)
+    loads[2].wait()
+    gring.start()
+    for load in loads[3:9]:
+        load.wait()
+    for total in outs:
+        total.early()
     n2, inv2 = rms_parts(r1_ref[...])
     d_h2 = dh2_ref[...]
     ggf_ref[...] = jnp.sum(d_h2 * n2, axis=0, keepdims=True)
     d_r1[...] = dy_ref[...].astype(f32) + rms_back(d_h2 * gf_ref[...], n2, inv2)
-    da_ref[...] = d_r1[...].astype(bf16)
+    da[...] = d_r1[...].astype(bf16)
+    swaps = [copies.start_to_core(58, mix_ref, mxc.at[theirs])]
+    for z in range(4):
+        cols = pl.ds(z * 256, 256)
+        h1c[mine, cols] = h1_ref[:, piece(z, core)]
+        dac[mine, cols] = da[:, piece(z, core)]
+        swaps.append(
+            copies.start_to_core(60 + 2 * z, h1_ref.at[:, piece(z, 1 - core)], h1c.at[theirs, cols])
+        )
+        swaps.append(
+            copies.start_to_core(61 + 2 * z, da.at[:, piece(z, 1 - core)], dac.at[theirs, cols])
+        )
+    mxc[mine] = mix_ref[...]
     mask_rows(starts_ref, 0, False, mask)
     mask_rows(starts_ref, 1, True, mask)
-    loads[0].wait()
+    load_wo.wait()
     for g in range(KV):
         cols = slice(g * GROUP_COLS, (g + 1) * GROUP_COLS)
-        d_o[:, cols] = nt(da_ref[...], wo[cols]).astype(bf16)
-    loads[1].wait()
-    gring.step2()
-    sums = [PlaneSum(copies, 0, half, part, l1, l2, l3, l4) for half in (0, 1)]
+        d_o[:, cols] = nt(da[...], wbuf[cols]).astype(bf16)
+    load_wq.start()
+    load_kva.wait()
+    sums = [PlaneSum(copies, 0, half, kva, *landings) for half in (0, 1)]
     for row in (0, 1):
         rows = slice(row * BLOCK, (row + 1) * BLOCK)
         for g in range(KV):
@@ -902,13 +974,13 @@
             dq_rows = nn(d_scores, kv_rows)[:, :HD] * SCALE
             dq[rows, cols] = unstacked(dq_rows.astype(bf16))
             dkv = tn(d_scores, q_rows * jnp.asarray(SCALE, bf16)) + tn(probs.astype(bf16), do_rows)
-            part[4 * row : 4 * row + 4, :, :, lanes] = dkv.astype(bf16).reshape(
+            kva[4 * row : 4 * row + 4, :, :, lanes] = dkv.astype(bf16).reshape(
                 4, 4, BLOCK, KV_COLS
             )
-        sums[row].step1()
+        sums[row].far()
+        sums[row].early()
         if row == 0:
-            gfull[gring.i] = gring.finish()[...]
-            gback.step1()
+            gring.late()
     means = head_means()
     cosine, sine = cos_ref[...], sin_ref[...]
 
@@ -917,28 +989,37 @@
         value, gain = turned_back(
             dq[:, cols].astype(f32), raw_ref[:, cols], qg_ref[...], cosine, sine, means
         )
-        dqkv_ref[:, cols] = value.astype(bf16)
+        dqc[mine, cols] = value.astype(bf16)
         return gain
 
     gain = queries(0)
     for g in range(1, KV):
         gain += queries(g)
     gq_ref[...] = gain
+    swaps.append(
+        copies.start_to_core(
+            68, dqc.at[mine, pl.ds(0, q_cols)], dqc.at[theirs, pl.ds(0, q_cols)]
+        )
+    )
     for total in sums:
-        total.step2()
-    gback.step2()
-    loads[2].wait()
+        total.late()
+    gboth[gring.i, place] = gring.finish()[...]
+    gback.step1()
+    for total in outs:
+        total.late()
+    load_wq.wait()
+    load_wkv.wait()
     tile = 512
     for n in range(width // tile):
         cols = slice(n * tile, (n + 1) * tile)
-        d_h1[:, cols] = nt(dqkv_ref[:, :q_cols], wqkv[cols, :q_cols])
+        d_h1[:, cols] = nt(dqc[mine, :q_cols], wbuf[cols, :q_cols])
     for total in sums:
-        total.step3()
+        total.inner_start()
+    gback.step2()
     for total in sums:
-        total.step4()
-    gback.finish()
-    keep = pltpu.make_async_copy(gfull, gall_ref, lsem.at[4])
-    keep.start()
+        total.inner_late()
+    for total in outs:
+        total.inner_start()
     d_kv = jnp.concatenate([total.result().astype(bf16) for total in sums], 0)
     pieces = [d_kv[:, g * KV_COLS : g * KV_COLS + HD] for g in range(KV)]
     pieces += [d_kv[:, g * KV_COLS + HD : (g + 1) * KV_COLS] for g in range(KV)]
@@ -961,21 +1042,43 @@
     )
     lane = lax.broadcasted_iota(jnp.int32, gain2.shape, 1)
     gk_ref[...] = gain1 + jnp.where(lane < k_cols - GROUP_COLS, gain2, 0.0)
-    dqkv_ref[:, q_cols : q_cols + GROUP_COLS] = first.astype(bf16)
+    dqc[mine, q_cols : q_cols + GROUP_COLS] = first.astype(bf16)
     lane = lax.broadcasted_iota(jnp.int32, second.shape, 1)
-    dqkv_ref[:, q_cols + GROUP_COLS : q_cols + 2 * GROUP_COLS] = jnp.where(
+    dqc[mine, q_cols + GROUP_COLS : q_cols + 2 * GROUP_COLS] = jnp.where(
         lane < k_cols - GROUP_COLS,
         second.astype(bf16),
         d_kv[:, GROUP_COLS : 2 * GROUP_COLS],
     )
-    dqkv_ref[:, q_cols + 2 * GROUP_COLS :] = d_kv[:, 2 * GROUP_COLS :]
+    dqc[mine, q_cols + 2 * GROUP_COLS :] = d_kv[:, 2 * GROUP_COLS :]
+    kv_part = pl.ds(q_cols, 2 * k_cols)
+    swaps.append(copies.start_to_core(69, dqc.at[mine, kv_part], dqc.at[theirs, kv_part]))
+    gback.finish()
+    gswap = copies.start_to_core(59, gfull, gfull)
+    for total in outs:
+        total.inner_late()
     for n in range(width // tile):
         cols = slice(n * tile, (n + 1) * tile)
-        d_h1[:, cols] += nt(dqkv_ref[:, q_cols:], wqkv[cols, q_cols:])
+        d_h1[:, cols] += nt(dqc[mine, q_cols:], wkv[cols])
     n1, inv1 = rms_parts(x_ref[...].astype(f32))
     gga_ref[...] = jnp.sum(d_h1[...] * n1, axis=0, keepdims=True)
     gx_ref[...] = (d_r1[...] + rms_back(d_h1[...] * ga_ref[...], n1, inv1)).astype(bf16)
-    keep.wait()
+    for half in (0, 1):
+        rows = slice(half * BLOCK, (half + 1) * BLOCK)
+        y_ref[rows] = (r1_ref[rows] + outs[half].result()).astype(bf16)
+    gswap.wait_recv()
+    for swap in swaps:
+        swap.wait_recv()
+    keeps = [
+        pltpu.make_async_copy(gboth, gall_ref, lsem.at[4]),
+        pltpu.make_async_copy(h1c, h1_out, lsem.at[0]),
+        pltpu.make_async_copy(dac, da_out, lsem.at[1]),
+        pltpu.make_async_copy(dqc, dq_out, lsem.at[2]),
+        pltpu.make_async_copy(mxc, mx_out, lsem.at[3]),
+    ]
+    for keep in keeps:
+        keep.start()
+    for keep in keeps:
+        keep.wait()
     copies.finish()
 
 
@@ -987,10 +1090,13 @@
     x,
     q,
     raw,
+    h1,
+    mixed,
     kva,
     w_qkv,
     w_out,
     gsum,
+    outp,
     g_attn,
     g_ffn,
     q_gain,
@@ -1003,43 +1109,53 @@
     kv_cols = 2 * KV * HD
     vmem_spec = pl.BlockSpec(memory_space=pltpu.VMEM)
     any_spec = pl.BlockSpec(memory_space=pl.ANY)
+    both = (gsum.shape[0], 2 * gsum.shape[1], gsum.shape[2])
+    pair_shapes = [
+        (2 * count, width // 2),
+        (2 * count, width // 2),
+        (2 * count, q_cols + kv_cols),
+        (2 * count, q_cols),
+    ]
     return pl.pallas_call(
         rear_kernel,
         out_shape=(
             jax.ShapeDtypeStruct((count, width), bf16),
-            jax.ShapeDtypeStruct((count, q_cols + kv_cols), bf16),
             jax.ShapeDtypeStruct((count, width), bf16),
             jax.ShapeDtypeStruct((1, width), f32),
             jax.ShapeDtypeStruct((1, width), f32),
             jax.ShapeDtypeStruct((1, GROUP_COLS), f32),
             jax.ShapeDtypeStruct((1, GROUP_COLS), f32),
-            jax.ShapeDtypeStruct(gsum.shape, bf16),
+            jax.ShapeDtypeStruct(both, bf16),
+            *[jax.ShapeDtypeStruct(shape, bf16) for shape in pair_shapes],
         ),
         in_specs=[
             pl.BlockSpec(memory_space=pltpu.SMEM),
-            *[vmem_spec] * 6,
-            *[any_spec] * 4,
+            *[vmem_spec] * 8,
+            *[any_spec] * 5,
             *[vmem_spec] * 6,
         ],
-        out_specs=(*[vmem_spec] * 7, any_spec),
+        out_specs=(*[vmem_spec] * 6, *[any_spec] * 5),
         scratch_shapes=[
-            pltpu.VMEM((width, q_cols + kv_cols), bf16),
-            pltpu.VMEM((q_cols, width), bf16),
+            pltpu.VMEM((width, width), bf16),
+            pltpu.VMEM((width, kv_cols), bf16),
             pltpu.VMEM((8, 4, BLOCK, kv_cols), bf16),
-            pltpu.VMEM(gsum.shape, bf16),
             pltpu.VMEM(gsum.shape, bf16),
             pltpu.VMEM((2, gsum.shape[1] // 2, gsum.shape[2]), bf16),
             pltpu.VMEM((2, *gsum.shape[1:]), bf16),
-            pltpu.VMEM((8, 4, BLOCK, kv_cols), bf16),
+            pltpu.VMEM(both, bf16),
+            pltpu.VMEM((8, 4, BLOCK, width), bf16),
             pltpu.VMEM((2, BLOCK, 16 * BLOCK), f32),
             pltpu.VMEM((count, width), f32),
             pltpu.VMEM((count, q_cols), bf16),
             pltpu.VMEM((count, q_cols), bf16),
             pltpu.VMEM((count, width), f32),
+            pltpu.VMEM((count, width), bf16),
+            *[pltpu.VMEM(shape, bf16) for shape in pair_shapes],
             *sum_landings(kv_cols),
-            pltpu.SemaphoreType.DMA((24,)),
-            pltpu.SemaphoreType.DMA((24,)),
-            pltpu.SemaphoreType.DMA((5,)),
+            *sum_landings(width),
+            pltpu.SemaphoreType.DMA((70,)),
+            pltpu.SemaphoreType.DMA((70,)),
+            pltpu.SemaphoreType.DMA((15,)),
         ],
         compiler_params=pltpu.CompilerParams(
             collective_id=3, has_side_effects=True, vmem_limit_bytes=VMEM_BYTES
@@ -1053,10 +1169,13 @@
         x,
         q,
         raw,
+        h1,
+        mixed,
         kva,
         w_qkv,
         w_out,
         gsum,
+        outp,
         g_attn,
         g_ffn,
         q_gain,
@@ -1071,27 +1190,15 @@
 
 
 def projections_kernel(
-    h1_ref,
-    da_ref,
-    dqkv_ref,
-    mix_ref,
-    gain_ref,
-    gall_ref,
-    left_ref,
-    right_ref,
-    gain_out,
-    gboth_ref,
-    *scratch,
+    h1_ref, da_ref, dq_ref, mix_ref, gain_ref, left_ref, right_ref, gain_out, *scratch
 ):
-    (h1c, dac, dqc, mxc, gsum, gboth) = scratch[:6]
-    parts = scratch[6:9]
-    half1, full1, half2, full2, last = (scratch[9 + 3 * k : 12 + 3 * k] for k in range(5))
-    send, recv, lsem = scratch[24:]
-    tokens = h1_ref.shape[0]
+    gsum = scratch[0]
+    parts = scratch[1:4]
+    half1, full1, half2, full2, last = (scratch[4 + 3 * k : 7 + 3 * k] for k in range(5))
+    send, recv = scratch[19:]
     copies = Copies(send, recv)
     barrier = pltpu.get_barrier_semaphore()
     core = lax.axis_index("dp_1")
-    other = 1 - core
     for axis in CHIP_AXES:
         for by in (1, 2, 3):
             pl.semaphore_signal(
@@ -1100,52 +1207,28 @@
                 device_id={axis: shift(lax.axis_index(axis), by)},
                 device_id_type=MESH,
             )
-    pl.semaphore_signal(barrier, inc=1, device_id={"dp_1": other}, device_id_type=MESH)
+    pl.semaphore_signal(barrier, inc=1, device_id={"dp_1": 1 - core}, device_id_type=MESH)
     pl.semaphore_wait(barrier, 10)
-
-    to_other = copies.start_to_core
-    mine, theirs = pl.ds(0, tokens), pl.ds(tokens, tokens)
-
-    def piece(z, which):
-        return pl.ds(pl.multiple_of(z * 512 + which * 256, 256), 256)
-
-    moves = [
-        to_other(0, dqkv_ref, dqc.at[theirs]),
-        to_other(1, mix_ref, mxc.at[theirs]),
-    ]
-    for z in range(4):
-        cols = pl.ds(z * 256, 256)
-        moves.append(to_other(2 + 2 * z, h1_ref.at[:, piece(z, other)], h1c.at[theirs, cols]))
-        moves.append(to_other(3 + 2 * z, da_ref.at[:, piece(z, other)], dac.at[theirs, cols]))
-    gain_move = to_other(10, gain_ref, gsum.at[3, core])
-    grows = gall_ref.shape[1]
-    place = gboth.at[:, pl.ds(pl.multiple_of(core * grows, 16), grows)]
-    gmove = to_other(53, gall_ref, place)
-    gload = pltpu.make_async_copy(gall_ref, place, lsem.at[0])
-    gload.start()
-    for z in range(4):
-        cols = pl.ds(z * 256, 256)
-        h1c[mine, cols] = h1_ref[:, piece(z, core)]
-        dac[mine, cols] = da_ref[:, piece(z, core)]
-    dqc[mine] = dqkv_ref[...]
-    mxc[mine] = mix_ref[...]
-    for move in moves:
-        move.wait_recv()
-
+    gain_move = copies.start_to_core(0, gain_ref, gsum.at[3, core])
     widths = [part.shape[4] for part in parts]
-    qkv_width = dqkv_ref.shape[1]
+    qkv_width = dq_ref.shape[1]
     columns = qkv_width + mix_ref.shape[1]
     split = qkv_width - widths[0]
     sources = (
-        ((h1c, dqc, 0, widths[0], 0),),
-        ((h1c, dqc, widths[0], split, 0), (dac, mxc, 0, widths[1] - split, split)),
-        ((dac, mxc, widths[1] - split, widths[2], 0),),
+        ((h1_ref, dq_ref, 0, widths[0], 0),),
+        ((h1_ref, dq_ref, widths[0], split, 0), (da_ref, mix_ref, 0, widths[1] - split, split)),
+        ((da_ref, mix_ref, widths[1] - split, widths[2], 0),),
     )
-
-    @pl.loop(0, 4)
-    def _(z):
-        cols = pl.ds(pl.multiple_of(z * 256, 256), 256)
-        for k in range(3):
+    base = 10
+    rings = [
+        RingSum(copies, base + 6 * k, AXIS_ORDERS[k][0], parts[k], half1[k], full1[k])
+        for k in range(3)
+    ]
+    for k in (2, 1, 0):
+
+        @pl.loop(0, 4)
+        def _(z, k=k):
+            cols = pl.ds(pl.multiple_of(z * 256, 256), 256)
             for lhs, rhs, first, width, place in sources[k]:
                 value = tn(lhs[:, cols], rhs[:, first : first + width]).astype(bf16)
                 value = value.reshape(4, 4, 16, width)
@@ -1158,13 +1241,15 @@
                     for y in range(4):
                         parts[2][:, z, y, :, to] = value[y]
 
+        rings[k].start()
+
     def gain_step(k, axis, value):
         i = lax.axis_index(axis)
         gsum[k, i] = value
         out = []
         for n, by in enumerate((1, 2, 3)):
             src = gsum.at[k, i]
-            out.append(copies.start(11 + 3 * k + n, src, src, axis, by))
+            out.append(copies.start(1 + 3 * k + n, src, src, axis, by))
         return out
 
     def gain_total(k, moves):
@@ -1172,70 +1257,55 @@
             move.wait_recv()
         return gsum[k, 0] + gsum[k, 1] + gsum[k, 2] + gsum[k, 3]
 
-    base = 20
-    rings = [
-        RingSum(copies, base + 4 * k, AXIS_ORDERS[k][0], parts[k], half1[k], full1[k])
-        for k in range(3)
-    ]
-    for ring in rings:
-        ring.step1()
-    gmove.wait_recv()
-    gload.wait()
-    gkeep = pltpu.make_async_copy(gboth, gboth_ref, lsem.at[1])
-    gkeep.start()
     gain_move.wait_recv()
     gsum[3, core] = gain_ref[...]
     total = gsum[3, 0] + gsum[3, 1]
     gmoves = gain_step(0, CHIP_AXES[0], total)
-    for ring in rings:
-        ring.step2()
+    for k in (2, 1, 0):
+        rings[k].late()
     gmoves = gain_step(1, CHIP_AXES[1], gain_total(0, gmoves))
-    owns = [ring.finish() for ring in rings]
-    rings = [
-        RingSum(copies, base + 12 + 4 * k, AXIS_ORDERS[k][1], owns[k], half2[k], full2[k])
-        for k in range(3)
-    ]
-    for ring in rings:
-        ring.step1()
+    owns = [None] * 3
+    rings2 = [None] * 3
+    for k in (2, 1, 0):
+        owns[k] = rings[k].finish()
+        rings2[k] = RingSum(
+            copies, base + 18 + 6 * k, AXIS_ORDERS[k][1], owns[k], half2[k], full2[k]
+        )
+        rings2[k].start()
     gmoves = gain_step(2, CHIP_AXES[2], gain_total(1, gmoves))
-    for ring in rings:
-        ring.step2()
+    for k in (2, 1, 0):
+        rings2[k].late()
     gain_out[...] = gain_total(2, gmoves)
-    owns = [ring.finish() for ring in rings]
-    ends = []
-    for k in range(3):
+    ends = [None] * 3
+    for k in (2, 1, 0):
+        owns[k] = rings2[k].finish()
         axis = AXIS_ORDERS[k][2]
         i = lax.axis_index(axis)
-        for n, by in enumerate((1, 2, 3)):
-            ends.append(
-                copies.start(
-                    base + 24 + 3 * k + n, owns[k].at[shift(i, by)], last[k].at[n], axis, by
-                )
-            )
-    for end in ends:
-        end.wait_recv()
-    place = 0
-    for k in range(3):
+        ends[k] = [
+            copies.start(base + 36 + 3 * k + n, owns[k].at[shift(i, by)], last[k].at[n], axis, by)
+            for n, by in enumerate((1, 2, 3))
+        ]
+    starts = (0, widths[0], widths[0] + widths[1])
+    for k in (2, 1, 0):
         i = lax.axis_index(AXIS_ORDERS[k][2])
+        for end in ends[k]:
+            end.wait_recv()
         value = owns[k][i].astype(f32)
         for n in range(3):
             value = value + last[k][n].astype(f32)
+        place = starts[k]
         for ref, first, last_col in ((left_ref, 0, qkv_width), (right_ref, qkv_width, columns)):
             low, high = max(first, place), min(last_col, place + widths[k])
             if low < high:
                 ref[:, low - first : high - first] = value[:, low - place : high - place]
-        place += widths[k]
-    gkeep.wait()
     copies.finish()
 
 
-def projections(h1, d_attn, d_qkv, mixed, gains, gall):
-    tokens, qkv_width = d_qkv.shape
+def projections(h1, d_attn, d_qkv, mixed, gains):
+    qkv_width = d_qkv.shape[1]
     columns = qkv_width + mixed.shape[1]
     widths = (1536, 1536, columns - 3072)
-    any_spec = pl.BlockSpec(memory_space=pl.ANY)
     vmem_spec = pl.BlockSpec(memory_space=pltpu.VMEM)
-    rows = h1.shape[1] // 2
 
     def each(make):
         return [pltpu.VMEM(make(width), bf16) for width in widths]
@@ -1246,32 +1316,25 @@
             jax.ShapeDtypeStruct((16, qkv_width), f32),
             jax.ShapeDtypeStruct((16, mixed.shape[1]), f32),
             jax.ShapeDtypeStruct(gains.shape, f32),
-            jax.ShapeDtypeStruct((gall.shape[0], 2 * gall.shape[1], gall.shape[2]), bf16),
         ),
-        in_specs=[*[vmem_spec] * 5, any_spec],
-        out_specs=(vmem_spec, vmem_spec, vmem_spec, any_spec),
+        in_specs=[vmem_spec] * 5,
+        out_specs=(vmem_spec,) * 3,
         scratch_shapes=[
-            pltpu.VMEM((2 * tokens, rows), bf16),
-            pltpu.VMEM((2 * tokens, rows), bf16),
-            pltpu.VMEM((2 * tokens, qkv_width), bf16),
-            pltpu.VMEM((2 * tokens, mixed.shape[1]), bf16),
             pltpu.VMEM((4, 4, *gains.shape), f32),
-            pltpu.VMEM((gall.shape[0], 2 * gall.shape[1], gall.shape[2]), bf16),
             *each(lambda w: (4, 4, 4, 16, w)),
             *each(lambda w: (2, 2, 4, 16, w)),
             *each(lambda w: (2, 4, 4, 16, w)),
             *each(lambda w: (2, 2, 16, w)),
             *each(lambda w: (2, 4, 16, w)),
             *each(lambda w: (3, 16, w)),
-            pltpu.SemaphoreType.DMA((54,)),
-            pltpu.SemaphoreType.DMA((54,)),
-            pltpu.SemaphoreType.DMA((2,)),
+            pltpu.SemaphoreType.DMA((55,)),
+            pltpu.SemaphoreType.DMA((55,)),
         ],
         compiler_params=pltpu.CompilerParams(
             collective_id=4, has_side_effects=True, vmem_limit_bytes=VMEM_BYTES
         ),
         name="projections",
-    )(h1, d_attn, d_qkv, mixed, gains, gall)
+    )(h1, d_attn, d_qkv, mixed, gains)
 
 
 def widen_kernel(g_ref, gin_ref, gdn_ref):
@@ -1327,10 +1390,7 @@
         doc_starts, x, w_qkv, w_out, ga, gf, qg, kg, cosine, sine, d_out
     )
     outp, d_h2, gsum = ffn(h2.reshape(rows, tok, width), dy_all, w_ffn_in, w_ffn_out)
-    ffn_sum = lax.psum_scatter(
-        outp.reshape(n_seq * n_head * count, width), ("seq", "head"), scatter_dimension=0, tiled=True
-    )
-    d_attn, d_qkv, grad_x, grad_gattn, grad_gffn, grad_qgain, grad_kgain, gall = rear(
+    output, grad_x, grad_gattn, grad_gffn, grad_qgain, grad_kgain, gboth, *pairs = rear(
         doc_starts,
         d_h2.reshape(count, width),
         r1,
@@ -1338,10 +1398,13 @@
         x,
         q,
         raw,
+        h1,
+        mixed,
         kva,
         w_qkv,
         w_out,
         gsum,
+        outp,
         ga,
         gf,
         qg,
@@ -1351,10 +1414,9 @@
     )
     gains = jnp.concatenate([grad_gattn, grad_gffn, grad_qgain, grad_kgain], 1)[0]
     gains = jnp.pad(gains, (0, 40 * 128 - gains.shape[0])).reshape(40, 128)
-    grad_qkv, grad_out, gains, gboth = projections(h1, d_attn, d_qkv, mixed, gains, gall)
+    grad_qkv, grad_out, gains = projections(*pairs, gains)
     grad_in, grad_down = widen(gboth, w_ffn_out.shape[0])
     gains = gains.reshape(-1)
-    output = (r1 + ffn_sum.astype(f32)).astype(bf16)
     heads = gains[2 * width : 2 * width + 2 * GROUP_COLS].reshape(2, PER_GROUP, HD).sum(1)
     return (
         output.reshape(rows, tok, width),

time: 370 us -> 336 us (0.908)
  Pallas kernels: 338 us -> 318 us
  between operations: 14.3 us -> 0.9 us
    pallas_call x1, Pallas kernels: 63.5 us -> 54.8 us  [projections(): pl.pallas_call(projections_kernel, out_shape=(jax.ShapeDtypeStruct((16, q...]
    pallas_call x1, Pallas kernels: 83.9 us -> 76.6 us  [rear(): pl.pallas_call(rear_kernel, out_shape=(jax.ShapeDtypeStruct((count, width...]
    pallas_call x1, Pallas kernels: 107 us -> 103 us  [ffn(): pl.pallas_call(ffn_kernel, out_shape=(jax.ShapeDtypeStruct((8, 4, BLOCK,...]
  transfers between devices with their start and end apart: 1 -> 0, of which waited for: 0 -> 0; matrix products, arithmetic and copies ran while one was open for 1% -> 0% of each run, Pallas kernels for 43% -> 0%
where the time goes in v3:
time: 336 us; the launch traced here: 330 us
  Pallas kernels  318 us (95%)
  local copies, waits for them, and re-layouts  8.79 us (3%)
    pallas_call x1, Pallas kernels, ffn(): pl.pallas_call(ffn_kernel, out_shape=(jax.ShapeDtypeStruct((8, 4, BLOCK,...  103 us
    pallas_call x1, Pallas kernels, rear(): pl.pallas_call(rear_kernel, out_shape=(jax.ShapeDtypeStruct((count, width...  76.6 us
    pallas_call x1, Pallas kernels, front(): pl.pallas_call(front_kernel, out_shape=(jax.ShapeDtypeStruct((count, widt...  76.3 us
    pallas_call x1, Pallas kernels, projections(): pl.pallas_call(projections_kernel, out_shape=(jax.ShapeDtypeStruct((16, q...  54.8 us
    pallas_call x1, Pallas kernels, widen(): pl.pallas_call(widen_kernel, grid=(tiles,), out_shape=(jax.ShapeDtypeStru...  7.5 us

profile of v3, /device:TPU:0, one launch (start us, length us, event | category | flops | bytes accessed | tf_op | source)
XLA Modules:
  0.0 330.0 jit_solution(18363249176233245425)
XLA Ops:
  0.7 0.7 tile.4
  1.3 0.6 broadcast_in_dim_tile.6.qg_ref
  2.0 0.7 tile.5
  2.6 0.6 broadcast_in_dim_tile.7.kg_ref
  3.3 1.2 fusion
  4.5 76.3 %front.1 = (bf16[128,2048]{1,0:T(8,128)(2,1)}, f32[128,2688]{1,0:T(8,128)}, bf16[128,1792]{1,0:T(8,128)(2,1)}, bf16[8,4,64,896]{3,2,1,0:T(8,128)(2,1)}, bf16[128...) custom-call(s32[2,4]{1,0:T(2,128)} %starts_ref.3, ...), custom_call_target="tpu_custom_call" | custom-call | tf_op jit(solution)/shard_map/front/pallas_call | solution.py:779
  80.9 102.9 %ffn.1 = (bf16[8,4,64,2048]{3,2,1,0:T(8,128)(2,1)}, f32[2,64,2048]{2,1,0:T(8,128)}, bf16[4,672,512]{2,1,0:T(8,128)(2,1)}) custom-call(bf16[2,64,2048]{2,1,0:T(8,128)(2,1)} %bitcast.23, bf16[8,4,64,2048]{3,2,1,0:T(8,128)(2,1)} %get-tuple-element.38.dy_ref, bf16[448,2,2048]{2,1,0:T(2,128)(2,1)} %win_ref.1, bf16[448,2048]{1,0:T(8,128)(2,1)} %wdn_ref.1), custom_call_target="tpu_custom_call" | custom-call | tf_op jit(solution)/shard_map/ffn/pallas_call | solution.py:486
  183.8 76.6 %rear.1 = (bf16[128,2048]{1,0:T(8,128)(2,1)}, bf16[128,2048]{1,0:T(8,128)(2,1)}, f32[1,2048]{1,0:T(1,128)}, f32[1,2048]{1,0:T(1,128)}, f32[1,256]{1,0:T(1,128)},...) custom-call(s32[2,4]{1,0:T(2,128)} %starts_ref.3, ...), custom_call_target="tpu_custom_call" | custom-call | tf_op jit(solution)/shard_map/rear/pallas_call | solution.py:1119
  260.4 0.8 maximum_reduce_fusion
  261.2 0.6 pad_bitcast_fusion.gain_ref
  261.8 0.0 copy-start.1
  261.8 54.8 %projections.1 = (f32[16,2688]{1,0:T(8,128)}, f32[16,1792]{1,0:T(8,128)}, f32[40,128]{1,0:T(8,128)}) custom-call(bf16[256,1024]{1,0:T(8,128)(2,1)} %get-tuple-element.50.h1_ref, bf16[256,1024]{1,0:T(8,128)(2,1)} %get-tuple-element.51.da_ref, bf16[256,2688]{1,0:T(8,128)(2,1)} %get-tuple-element.52.dq_ref, bf16[256,1792]{1,0:T(8,128)(2,1)} %get-tuple-element.53.mix_ref, ...), custom_call_target="tpu_custom_call" | custom-call | tf_op jit(solution)/shard_map/projections/pallas_call | solution.py:1313
  316.7 0.0 copy-start
  316.7 0.7 slice.26
  317.4 1.3 slice_bitcast_fusion
  318.8 0.1 reshape.92
  318.9 0.5 slice_bitcast_fusion.2
  319.4 0.0 copy-start.2
  319.4 0.0 copy-start.3
  319.4 7.5 %widen.1 = (f32[448,2,2048]{2,1,0:T(2,128)}, f32[448,2048]{1,0:T(8,128)}) custom-call(bf16[4,1344,512]{2,1,0:T(8,128)(2,1)} %get-tuple-element.60.g_ref), custom_call_target="tpu_custom_call" | custom-call | tf_op jit(solution)/shard_map/widen/pallas_call | solution.py:1349
  326.9 0.0 copy-done.1
  326.9 0.8 copy.25
  327.7 0.0 copy-done
  327.7 0.8 copy.26
  328.5 0.0 copy-done.2
  328.5 0.7 copy.27
  329.2 0.0 copy-done.3
  329.2 0.6 copy.28
  (3 shorter events, 0.0 us)
Async XLA Ops:
  261.8 65.1 %copy-start.1 = (bf16[128,2048]{1,0:T(8,128)(2,1)S(1)}, bf16[128,2048]{1,0:T(8,128)(2,1)}, u32[]{:S(2)}) copy-start(bf16[128,2048]{1,0:T(8,128)(2,1)} %get-tuple-element.48) | copy-start | bytes 1572868
  316.7 11.0 %copy-start = (bf16[128,2048]{1,0:T(8,128)(2,1)S(1)}, bf16[128,2048]{1,0:T(8,128)(2,1)}, u32[]{:S(2)}) copy-start(bf16[128,2048]{1,0:T(8,128)(2,1)} %get-tuple-element.49) | copy-start | bytes 1572868
  319.4 9.1 %copy-start.2 = (f32[16,2688]{1,0:T(8,128)S(1)}, f32[16,2688]{1,0:T(8,128)}, u32[]{:S(2)}) copy-start(f32[16,2688]{1,0:T(8,128)} %get-tuple-element.84) | copy-start | bytes 516100
  319.4 9.8 %copy-start.3 = (f32[16,1792]{1,0:T(8,128)S(1)}, f32[16,1792]{1,0:T(8,128)}, u32[]{:S(2)}) copy-start(f32[16,1792]{1,0:T(8,128)} %get-tuple-element.59) | copy-start | bytes 344068
